TPU v7x, 32 devices: a whole 2x2x4 slice. The times are simulated.
32 devices in a mesh: row: 4 (over y, x), col: 8 (over z, core).
Axes of the slice: x: 2, y: 2, z: 4, core: 2. Of those that a mesh axis runs over, the one named last changes fastest.
Arguments:
- data: bfloat16 [4, 8, 32, 1024, 128], P('row', 'col'), may hold values from -6 to 6
- real_index: int32 [4, 8, 2, 2], P('row', 'col'), may hold values from 0 to 31
- latent_seed: int32 [4, 8, 2, 2], P('row', 'col'), may hold values from 0 to 255
- latent_bank: float32 [256, 128], replicated, may hold values from -6 to 6
- g_in: float32 [4, 8, 128, 128], P('row', 'col'), may hold values from -0.5 to 0.5
- g_base: float32 [4, 8, 1024, 128], P('row', 'col'), may hold values from -6 to 6
- g_one: float32 [4, 8, 128, 128], P('row', 'col'), may hold values from -0.5 to 0.5
- g_two: float32 [4, 8, 128, 128], P('row', 'col'), may hold values from -0.5 to 0.5
- d_one: float32 [4, 8, 128, 128], P('row', 'col'), may hold values from -0.5 to 0.5
- d_two: float32 [4, 8, 128, 128], P('row', 'col'), may hold values from -0.5 to 0.5
- d_out: float32 [4, 8, 128], P('row', 'col'), may hold values from -0.5 to 0.5
Outputs:
- new_g_in: float32 [4, 8, 128, 128], P('row', 'col')
- new_g_base: float32 [4, 8, 1024, 128], P('row', 'col')
- new_g_one: float32 [4, 8, 128, 128], P('row', 'col')
- new_g_two: float32 [4, 8, 128, 128], P('row', 'col')
- new_d_one: float32 [4, 8, 128, 128], P('row', 'col')
- new_d_two: float32 [4, 8, 128, 128], P('row', 'col')
- new_d_out: float32 [4, 8, 128], P('row', 'col')
- verdicts: float32 [4, 8, 2, 12], P('row', 'col')
All inputs are finite; a program needn't handle non-finite values.
Results may differ from a plain program's by a relative error of at most 0.0028.
Values may be sent and summed in bfloat16 or wider, within the bound.
A program may use at most 128 MiB of HBM per device.

v0:
```python
import jax
import jax.numpy as jnp
from jax import lax
from jax.sharding import PartitionSpec as P

STEPS = 2


learn_rate = 0.05
base_rate = 0.1


def padded(block, sides, width):
    for axis, dim in sides:
        count = lax.axis_size(axis)
        forward = [(i, i + 1) for i in range(count - 1)]
        forward.append((count - 1, 0))
        backward = [(target, source) for source, target in forward]
        low = lax.ppermute(
            lax.slice_in_dim(block, block.shape[dim] - width, None, axis=dim), axis, forward
        )
        high = lax.ppermute(lax.slice_in_dim(block, 0, width, axis=dim), axis, backward)
        block = jnp.concatenate([low, block, high], axis=dim)
    return block


def shifted_2(block, axis, distance):
    devices = range(lax.axis_size(axis))
    route = [((i - distance) % len(devices), i) for i in devices]
    return lax.ppermute(block, axis, route)


def matmul(left_side, right_side):
    return jnp.dot(left_side, right_side, preferred_element_type=jnp.float32)


def rows_matmul(left_side, right_side):
    return lax.dot_general(
        left_side, right_side, (((0,), (0,)), ((), ())), preferred_element_type=jnp.float32
    )


def silu_slope(values):
    sigmoid_part = jax.nn.sigmoid(values)
    return sigmoid_part * (1.0 + values * (1.0 - sigmoid_part))


def flatten_all(members):
    return jnp.concatenate([member.reshape(-1) for member in members], axis=0)


def split_all(flat, shapes):
    pieces = []
    offset = 0
    for shape in shapes:
        length = 1
        for extent in shape:
            length = length * extent
        pieces.append(flat[offset : offset + length].reshape(shape))
        offset = offset + length
    return tuple(pieces)


def generate(latent, weights):
    w_in, w_base, w_one, w_two = weights
    shifted = matmul(latent, w_in)
    batch_count = latent.shape[0]
    places, channels = w_base.shape
    gen_pre = (w_base.astype(jnp.float32)[None] + shifted[:, None, :]).reshape(
        batch_count * places, channels
    )
    hidden = jax.nn.silu(gen_pre).astype(jnp.bfloat16)
    middle_pre = matmul(hidden, w_one)
    middle = jax.nn.silu(middle_pre).astype(jnp.bfloat16)
    own_fakes = (
        lax.optimization_barrier(hidden).astype(jnp.float32) + matmul(middle, w_two)
    ).astype(jnp.bfloat16)
    return (own_fakes, (gen_pre, hidden, middle_pre, middle))


def generator_grads(cotangent, stored, latent, weights):
    gen_pre, hidden, middle_pre, middle = stored
    w_in, w_base, w_one, w_two = weights
    repeats = cotangent.shape[0] // hidden.shape[0]
    grad_two = rows_matmul(jnp.tile(middle, (repeats, 1)), cotangent)
    inner_term = matmul(cotangent, w_two.T) * jnp.tile(silu_slope(middle_pre), (repeats, 1))
    inner_half = inner_term.astype(jnp.bfloat16)
    grad_one = rows_matmul(jnp.tile(hidden, (repeats, 1)), inner_half)
    outer_term = (cotangent.astype(jnp.float32) + matmul(inner_half, w_one.T)) * jnp.tile(
        silu_slope(gen_pre), (repeats, 1)
    )
    batch_count = latent.shape[0]
    places, channels = w_base.shape
    outer_term = outer_term.reshape(repeats, batch_count, places, channels)
    grad_base = jnp.sum(outer_term, axis=(0, 1))
    grad_in = jnp.dot(
        latent.astype(jnp.float32).T,
        jnp.sum(outer_term, axis=(0, 2)),
        precision=lax.Precision.HIGHEST,
    )
    return (grad_in, grad_base, grad_one, grad_two)


def judge(images, d_one, d_two, d_out, batch_count):
    places = images.shape[0] // batch_count
    first_pre = matmul(images, d_one)
    first_act = jax.nn.silu(first_pre).astype(jnp.bfloat16)
    summed = images.astype(jnp.float32) + matmul(first_act, d_two)
    feature = jax.nn.silu(summed)
    verdict = jnp.sum(feature * d_out[None, :], axis=1).reshape(batch_count, places).mean(axis=1)
    return (verdict, (first_pre, first_act, summed, feature))


def judge_back(slopes, stored, d_two, d_out, places):
    first_pre, first_act, summed, feature = stored
    weight_rows = jnp.repeat(slopes / places, places)
    outer_term = weight_rows[:, None] * d_out[None, :] * silu_slope(summed)
    outer_half = outer_term.astype(jnp.bfloat16)
    inner_half = (matmul(outer_half, d_two.T) * silu_slope(first_pre)).astype(jnp.bfloat16)
    return (weight_rows, outer_term, outer_half, inner_half)


def add_grads(first_set, second_set):
    return tuple(
        (first_part + second_part for first_part, second_part in zip(first_set, second_set))
    )


def on_device(
    data, real_index, latent_seed, latent_bank, g_in, g_base, g_one, g_two, d_one, d_two, d_out
):
    places = data.shape[3]
    channels = data.shape[4]
    batch_count = latent_seed.shape[3]
    reals_count = real_index.shape[3]
    fake_count = 5 * batch_count
    step_sizes = [
        learn_rate,
        base_rate * places,
        learn_rate,
        learn_rate,
        learn_rate,
        learn_rate,
        learn_rate,
    ]
    bank_half = latent_bank.astype(jnp.bfloat16)
    params = [member[0, 0] for member in (g_in, g_base, g_one, g_two, d_one, d_two, d_out)]
    verdict_list = []
    for step_index in range(STEPS):
        chosen = (
            latent_seed[0, 0, step_index][:, None] == jnp.arange(bank_half.shape[0])[None, :]
        ).astype(jnp.bfloat16)
        latent = matmul(chosen, bank_half).astype(jnp.bfloat16)
        real_rows = jnp.take(data[0, 0], real_index[0, 0, step_index], axis=0).reshape(
            reals_count * places, channels
        )
        halves = [member.astype(jnp.bfloat16) for member in params[:6]]
        gen_half = tuple(halves[:4])
        grad_shapes = [member.shape for member in params[:4]]
        own_fakes, stored = generate(latent, gen_half)
        neighbours = []
        model_members = (latent,) + gen_half
        model_shapes = [member.shape for member in model_members]
        packed = flatten_all(model_members)[None, None]
        beside_all = padded(packed, (("row", 0), ("col", 1)), 1)
        judged = [own_fakes]
        for row_place, col_place in ((0, 1), (2, 1), (1, 0), (1, 2)):
            unpacked = split_all(beside_all[row_place, col_place], model_shapes)
            their_latent = unpacked[0]
            their_weights = tuple(unpacked[1:])
            their_fakes, their_stored = generate(their_latent, their_weights)
            judged.append(their_fakes)
            neighbours.append((their_latent, their_weights, their_stored))
        images = jnp.concatenate(judged + [real_rows], axis=0)
        verdict, disc_stored = judge(
            images, halves[4], halves[5], params[6], fake_count + reals_count
        )
        verdict_list.append(verdict)
        fake_verdict = verdict[:fake_count]
        real_verdict = verdict[fake_count:]
        disc_slope = jnp.concatenate([jax.nn.sigmoid(fake_verdict), -jax.nn.sigmoid(-real_verdict)])
        weight_rows, outer_term, outer_half, inner_half = judge_back(
            disc_slope, disc_stored, halves[5], params[6], places
        )
        grad_out = jnp.sum(disc_stored[3] * weight_rows[:, None], axis=0)
        grad_dtwo = rows_matmul(disc_stored[1], outer_half)
        grad_done = rows_matmul(images, inner_half)
        fake_rows = fake_count * places
        fake_stored = tuple((member[:fake_rows] for member in disc_stored))
        gen_slope = -jax.nn.sigmoid(-fake_verdict)
        unused, gen_outer, gen_half_out, gen_inner = judge_back(
            gen_slope, fake_stored, halves[5], params[6], places
        )
        returned = (gen_outer + matmul(gen_inner, halves[4].T)).astype(jnp.bfloat16)
        returned = returned.reshape(5, batch_count * places, channels)
        gen_grads = generator_grads(returned[0], stored, latent, gen_half)
        for which_slot, by_value in ((1, -1), (2, 1)):
            their_latent, their_weights, their_stored = neighbours[which_slot - 1]
            their_grads = generator_grads(
                returned[which_slot], their_stored, their_latent, their_weights
            )
            moved = shifted_2(flatten_all(their_grads), "row", by_value)
            gen_grads = add_grads(gen_grads, split_all(moved, grad_shapes))
        for which_slot, by_value in ((3, -1), (4, 1)):
            their_latent, their_weights, their_stored = neighbours[which_slot - 1]
            their_grads = generator_grads(
                returned[which_slot], their_stored, their_latent, their_weights
            )
            moved = shifted_2(flatten_all(their_grads), "col", by_value)
            gen_grads = add_grads(gen_grads, split_all(moved, grad_shapes))
        all_grads = list(gen_grads) + [grad_done, grad_dtwo, grad_out]
        params = [
            member - step_size * grad
            for member, grad, step_size in zip(params, all_grads, step_sizes)
        ]
    verdicts = jnp.stack(verdict_list, axis=0)[None, None]
    finals = [member[None, None] for member in params]
    return (finals[0], finals[1], finals[2], finals[3], finals[4], finals[5], finals[6], verdicts)


def solution(mesh):
    return jax.shard_map(
        on_device,
        mesh=mesh,
        in_specs=(
            P("row", "col", None, None, None),
            P("row", "col", None, None),
            P("row", "col", None, None),
            P(),
            P("row", "col", None, None),
            P("row", "col", None, None),
            P("row", "col", None, None),
            P("row", "col", None, None),
            P("row", "col", None, None),
            P("row", "col", None, None),
            P("row", "col", None),
        ),
        out_specs=(
            P("row", "col", None, None),
            P("row", "col", None, None),
            P("row", "col", None, None),
            P("row", "col", None, None),
            P("row", "col", None, None),
            P("row", "col", None, None),
            P("row", "col", None),
            P("row", "col", None, None),
        ),
        check_vma=False,
    )
```

profile of v0, /device:TPU:13, one launch (start us, length us, event | category | flops | bytes accessed | tf_op | source)
XLA Modules:
  0.0 371.5 jit_solution(7793451429446265384)
XLA Ops:
  7.0 2.6 dynamic-update-slice.19
  10.7 4.9 %broadcast_in_dim.35 = bf16[1,1,180480]{2,0,1:T(2,128)(2,1)} reshape(bf16[180480]{0:T(1024)(128)(2,1)S(1)} %dynamic-update-slice.21) | data formatting | bytes 721920 | tf_op jit(solution)/shard_map/broadcast_in_dim | solution.py:164
  22.1 4.0 %gather_fusion = bf16[2,1024,128]{2,1,0:T(8,128)(2,1)S(1)} fusion(bf16[32,1024,128]{2,1,0:T(8,128)(2,1)} %bitcast.915, s32[1024]{0:T(1024)S(1)} %get-tuple-element.128), kind=kCustom, calls=%fused_computation.clone | custom fusion | bytes 1048584 | tf_op jit(solution)/shard_map/jit(_take)/gather | solution.py:154
  26.1 4.0 %gather_fusion.1 = bf16[2,1024,128]{2,1,0:T(8,128)(2,1)S(1)} fusion(bf16[32,1024,128]{2,1,0:T(8,128)(2,1)} %bitcast.916, s32[1024]{0:T(1024)S(1)} %get-tuple-element.127), kind=kCustom, calls=%fused_computation.1.clone | custom fusion | bytes 1048584 | tf_op jit(solution)/shard_map/jit(_take)/gather | solution.py:154
  35.9 12.4 %collective-permute-done.1 = bf16[1,1,180480]{2,0,1:T(2,128)(2,1)} collective-permute-done((bf16[1,1,180480]{2,0,1:T(2,128)(2,1)}, bf16[1,1,180480]{2,0,1:T(2,128)(2,1)}, u32[]{:S(2)}, u32[]{:S(2)}) %collective-permute-start.1) | collective-permute-done | bytes 360992 | tf_op jit(solution)/shard_map/ppermute | solution.py:22
  48.3 3.8 %pad_maximum_fusion = bf16[3,1,180480]{2,0,1:T(4,128)(2,1)S(1)} fusion(bf16[1,1,180480]{2,0,1:T(2,128)(2,1)} %collective-permute-done.1, bf16[1,1,180480]{2,0,1:T(2,128)(2,1)} %broadcast_in_dim.35, bf16[1,1,180480]{2,0,1:T(2,128)(2,1)} %collective-permute-done), kind=kLoop, calls=%fused_computation.128 | loop fusion | flops 3248640 | bytes 2165760 | tf_op jit(solution)/shard_map/concatenate | solution.py:23
  52.2 2.8 collective-permute-start.2
  68.2 15.6 %collective-permute-done.2 = bf16[3,1,180480]{2,0,1:T(4,128)(2,1)S(1)} collective-permute-done((bf16[3,1,180480]{2,0,1:T(4,128)(2,1)S(1)}, bf16[3,1,180480]{2,0,1:T(4,128)(2,1)S(1)}, u32[]{:S(2)}, u32[]{:S(2)}) %collective-permute-start.2) | collective-permute-done | bytes 1082912 | tf_op jit(solution)/shard_map/ppermute | solution.py:19
  93.8 5.6 %multiply_reduce_fusion.3 = (f32[12288]{0:T(1024)S(1)}, f32[12288,128]{1,0:T(8,128)}) fusion(f32[128]{0:T(128)S(1)} %bitcast.920, f32[12288,128]{1,0:T(8,128)S(1)} %fusion.335, bf16[12288,128]{1,0:T(8,128)(2,1)S(1)} %constant_dynamic-update-slice_fusion, f32[1,1,128,128]{3,2,1,0:T(8,128)S(1)} %copy-done.129), kind=kOutput, calls=%fused_computation.25 | convolution fusion | flops 423088128 | bytes 15843840 | tf_op jit(solution)/shard_map/dot_general | solution.py:34
  100.2 13.3 %fusion.3 = bf16[10240,128]{1,0:T(8,128)(2,1)} fusion(f32[12288,128]{1,0:T(8,128)} %copy-done.1, f32[12288,128]{1,0:T(8,128)} %get-tuple-element.124, f32[128]{0:T(128)} %bitcast.919, f32[10240]{0:T(1024)S(1)} %mul.579, f32[1,1,128,128]{3,2,1,0:T(8,128)} %param.22, f32[1,1,128,128]{3,2,1,0:T(8,128)S(1)} %copy-done.74), kind=kOutput, calls=%fused_computation.13 | convolution fusion | flops 710410240 | bytes 18564096 | tf_op jit(solution)/shard_map/dot_general | solution.py:34
  113.6 2.8 fusion.30
  126.4 8.5 %multiply_reduce_fusion.2 = (f32[128]{0:T(128)S(1)}, bf16[12288,128]{1,0:T(8,128)(2,1)}) fusion(f32[12288]{0:T(1024)S(1)} %mul.637, f32[12288,128]{1,0:T(8,128)} %get-tuple-element.124, f32[128]{0:T(128)S(1)} %bitcast.921), kind=kLoop, calls=%fused_computation.19 | loop fusion | flops 20447104 | bytes 9487360 | tf_op jit(solution)/shard_map/reduce_sum | solution.py:185
  134.9 7.1 %fusion.60 = f32[128,128]{1,0:T(8,128)} fusion(bf16[12288,128]{1,0:T(8,128)(2,1)S(1)} %constant_dynamic-update-slice_fusion, bf16[12288,128]{1,0:T(8,128)(2,1)} %get-tuple-element.66, f32[12288,128]{1,0:T(8,128)} %copy-done.1, f32[1,1,128,128]{3,2,1,0:T(8,128)S(1)} %copy-done.74, f32[1,1,128,128]{3,2,1,0:T(8,128)} %param.22), kind=kOutput, calls=%fused_computation.138 | convolution fusion | flops 819494912 | bytes 12779520 | tf_op jit(solution)/shard_map/dot_general | solution.py:38
  147.1 2.4 collective-permute-start.4
  153.8 4.0 %collective-permute-start.7 = (f32[180224]{0:T(1024)S(1)}, f32[180224]{0:T(1024)S(1)}, u32[]{:S(2)}, u32[]{:S(2)}) collective-permute-start(f32[180224]{0:T(1024)S(1)} %pad_maximum_fusion.5), channel_id=1, source_target_pairs={{7,0},{0,1},{1,2},{2,3},{3,4},{4,5},{5,6},{6,7},{15,8},{8,9},{9,10... | collective-permute-start | bytes 2162696 | tf_op jit(solution)/shard_map/ppermute | solution.py:30
  158.4 2.5 fusion.56
  160.9 4.0 %collective-permute-done.4 = f32[180224]{0:T(1024)S(1)} collective-permute-done((f32[180224]{0:T(1024)S(1)}, f32[180224]{0:T(1024)S(1)}, u32[]{:S(2)}, u32[]{:S(2)}) %collective-permute-start.4) | collective-permute-done | bytes 720928 | tf_op jit(solution)/shard_map/ppermute | solution.py:30
  164.9 16.5 %collective-permute-done.5 = f32[180224]{0:T(1024)S(1)} collective-permute-done((f32[180224]{0:T(1024)S(1)}, f32[180224]{0:T(1024)S(1)}, u32[]{:S(2)}, u32[]{:S(2)}) %collective-permute-start.5) | collective-permute-done | bytes 720928 | tf_op jit(solution)/shard_map/ppermute | solution.py:30
  185.9 5.3 %dynamic-update-slice.8 = bf16[180480]{0:T(1024)(128)(2,1)} dynamic-update-slice(bf16[180480]{0:T(1024)(128)(2,1)} %dynamic-update-slice.7, bf16[131072]{0:T(1024)(128)(2,1)S(1)} %get-tuple-element.57, s32[]{} %constant.115) | dynamic-update-slice | bytes 524292
  194.3 4.3 %broadcast_in_dim.37 = bf16[1,1,180480]{2,0,1:T(2,128)(2,1)S(1)} reshape(bf16[180480]{0:T(1024)(128)(2,1)} %dynamic-update-slice.10) | data formatting | bytes 721920 | tf_op jit(solution)/shard_map/broadcast_in_dim | solution.py:164
  203.9 12.3 %collective-permute-done.8 = bf16[1,1,180480]{2,0,1:T(2,128)(2,1)S(1)} collective-permute-done((bf16[1,1,180480]{2,0,1:T(2,128)(2,1)S(1)}, bf16[1,1,180480]{2,0,1:T(2,128)(2,1)S(1)}, u32[]{:S(2)}, u32[]{:S(2)}) %collective-permute-start.8) | collective-permute-done | bytes 360992 | tf_op jit(solution)/shard_map/ppermute | solution.py:19
  216.2 14.3 %collective-permute-done.9 = bf16[1,1,180480]{2,0,1:T(2,128)(2,1)S(1)} collective-permute-done((bf16[1,1,180480]{2,0,1:T(2,128)(2,1)S(1)}, bf16[1,1,180480]{2,0,1:T(2,128)(2,1)S(1)}, u32[]{:S(2)}, u32[]{:S(2)}) %collective-permute-start.9) | collective-permute-done | bytes 360992 | tf_op jit(solution)/shard_map/ppermute | solution.py:22
  230.5 2.5 pad_maximum_fusion.1
  243.0 24.3 %collective-permute-done.11 = bf16[3,1,180480]{2,0,1:T(4,128)(2,1)S(1)} collective-permute-done((bf16[3,1,180480]{2,0,1:T(4,128)(2,1)S(1)}, bf16[3,1,180480]{2,0,1:T(4,128)(2,1)S(1)}, u32[]{:S(2)}, u32[]{:S(2)}) %collective-permute-start.11) | collective-permute-done | bytes 1082912 | tf_op jit(solution)/shard_map/ppermute | solution.py:22
  276.4 6.0 %multiply_reduce_fusion.1 = (f32[12288]{0:T(1024)}, f32[12288,128]{1,0:T(8,128)}) fusion(f32[128]{0:T(128)S(1)} %copy-done.125, f32[128,128]{1,0:T(8,128)S(1)} %copy-done.133, f32[12288,128]{1,0:T(8,128)S(1)} %fusion.262, bf16[12288,128]{1,0:T(8,128)(2,1)S(1)} %constant_dynamic-update-slice_fusion.1), kind=kOutput, calls=%fused_computation.18 | convolution fusion | flops 423104512 | bytes 15843840 | tf_op jit(solution)/shard_map/dot_general | solution.py:34
  287.0 13.5 %fusion.5 = bf16[10240,128]{1,0:T(8,128)(2,1)} fusion(f32[12288,128]{1,0:T(8,128)} %copy-done, f32[12288,128]{1,0:T(8,128)} %get-tuple-element.126, f32[128]{0:T(128)} %multiply_subtract_fusion, f32[10240]{0:T(1024)} %mul.654, f32[128,128]{1,0:T(8,128)S(1)} %copy-done.75, f32[128,128]{1,0:T(8,128)} %fusion.56), kind=kOutput, calls=%fused_computation.15 | convolution fusion | flops 710443008 | bytes 18564096 | tf_op jit(solution)/shard_map/dot_general | solution.py:34
  300.5 2.9 fusion.46
  313.3 8.6 %multiply_reduce_fusion = (f32[128]{0:T(128)S(1)}, bf16[12288,128]{1,0:T(8,128)(2,1)}) fusion(f32[12288]{0:T(1024)S(1)} %mul.698, f32[12288,128]{1,0:T(8,128)} %get-tuple-element.126, f32[128]{0:T(128)S(1)} %copy-done.126), kind=kLoop, calls=%fused_computation.16 | loop fusion | flops 20447104 | bytes 9487360 | tf_op jit(solution)/shard_map/reduce_sum | solution.py:185
  322.4 7.1 %fusion.63 = f32[1,1,128,128]{3,2,1,0:T(8,128)} fusion(f32[128,128]{1,0:T(8,128)S(1)} %copy-done.76, bf16[12288,128]{1,0:T(8,128)(2,1)S(1)} %constant_dynamic-update-slice_fusion.1, bf16[12288,128]{1,0:T(8,128)(2,1)} %get-tuple-element.64, f32[12288,128]{1,0:T(8,128)} %copy-done, f32[128,128]{1,0:T(8,128)} %fusion.56), kind=kOutput, calls=%fused_computation.141 | convolution fusion | flops 819511296 | bytes 12779520 | tf_op jit(solution)/shard_map/dot_general | solution.py:38
  343.0 2.5 fusion.58
  345.5 6.2 %collective-permute-done.12 = f32[180224]{0:T(1024)S(1)} collective-permute-done((f32[180224]{0:T(1024)S(1)}, f32[180224]{0:T(1024)S(1)}, u32[]{:S(2)}, u32[]{:S(2)}) %collective-permute-start.12) | collective-permute-done | bytes 720928 | tf_op jit(solution)/shard_map/ppermute | solution.py:30
  351.7 16.4 %collective-permute-done.13 = f32[180224]{0:T(1024)S(1)} collective-permute-done((f32[180224]{0:T(1024)S(1)}, f32[180224]{0:T(1024)S(1)}, u32[]{:S(2)}, u32[]{:S(2)}) %collective-permute-start.13) | collective-permute-done | bytes 720928 | tf_op jit(solution)/shard_map/ppermute | solution.py:30
  (492 shorter events, 125.6 us)
Async XLA Ops:
  0.6 20.2 %copy-start.67 = (f32[1,1,128,128]{3,2,1,0:T(8,128)S(1)}, f32[1,1,128,128]{3,2,1,0:T(8,128)}, u32[]{:S(2)}) copy-start(f32[1,1,128,128]{3,2,1,0:T(8,128)} %param.19) | copy-start | bytes 196612
  0.6 21.4 %copy-start.124 = (s32[1,1,2,2]{3,2,1,0:T(2,128)S(1)}, s32[1,1,2,2]{3,2,1,0:T(2,128)}, u32[]{:S(2)}) copy-start(s32[1,1,2,2]{3,2,1,0:T(2,128)} %param.14) | copy-start | bytes 52
  6.3 24.8 %copy-start.107 = (bf16[2,128]{1,0:T(2,128)(2,1)}, bf16[2,128]{1,0:T(2,128)(2,1)S(1)}, u32[]{:S(2)}) copy-start(bf16[2,128]{1,0:T(2,128)(2,1)S(1)} %convolution_convert_fusion.1) | copy-start | bytes 1540
  15.6 20.4 %collective-permute-start = (bf16[1,1,180480]{2,0,1:T(2,128)(2,1)}, bf16[1,1,180480]{2,0,1:T(2,128)(2,1)}, u32[]{:S(2)}, u32[]{:S(2)}) collective-permute-start(bf16[1,1,180480]{2,0,1:T(2,128)(2,1)} %broadcast_in_dim.35), channel_id=1, source_target_pairs={{0,8},{8,16},{16,24},{24,0},{1,9},{9,17},{17,25},{25,1},{2,10},{10... | collective-permute-start | bytes 1082888 | tf_op jit(solution)/shard_map/ppermute | solution.py:19
  16.8 31.5 %collective-permute-start.1 = (bf16[1,1,180480]{2,0,1:T(2,128)(2,1)}, bf16[1,1,180480]{2,0,1:T(2,128)(2,1)}, u32[]{:S(2)}, u32[]{:S(2)}) collective-permute-start(bf16[1,1,180480]{2,0,1:T(2,128)(2,1)} %broadcast_in_dim.35), channel_id=1, source_target_pairs={{8,0},{16,8},{24,16},{0,24},{9,1},{17,9},{25,17},{1,25},{10,2},{18... | collective-permute-start | bytes 1082888 | tf_op jit(solution)/shard_map/ppermute | solution.py:22
  52.2 31.6 %collective-permute-start.2 = (bf16[3,1,180480]{2,0,1:T(4,128)(2,1)S(1)}, bf16[3,1,180480]{2,0,1:T(4,128)(2,1)S(1)}, u32[]{:S(2)}, u32[]{:S(2)}) collective-permute-start(bf16[3,1,180480]{2,0,1:T(4,128)(2,1)S(1)} %pad_maximum_fusion), channel_id=1, source_target_pairs={{0,1},{1,2},{2,3},{3,4},{4,5},{5,6},{6,7},{7,0},{8,9},{9,10},{10,1... | collective-permute-start | bytes 3248648 | tf_op jit(solution)/shard_map/ppermute | solution.py:19
  55.0 32.6 %collective-permute-start.3 = (bf16[3,1,180480]{2,0,1:T(4,128)(2,1)S(1)}, bf16[3,1,180480]{2,0,1:T(4,128)(2,1)S(1)}, u32[]{:S(2)}, u32[]{:S(2)}) collective-permute-start(bf16[3,1,180480]{2,0,1:T(4,128)(2,1)S(1)} %pad_maximum_fusion), channel_id=1, source_target_pairs={{1,0},{2,1},{3,2},{4,3},{5,4},{6,5},{7,6},{0,7},{9,8},{10,9},{11,1... | collective-permute-start | bytes 3248648 | tf_op jit(solution)/shard_map/ppermute | solution.py:22
  134.9 22.9 %copy-start.122 = (f32[128]{0:T(128)}, f32[128]{0:T(128)S(1)}, u32[]{:S(2)}) copy-start(f32[128]{0:T(128)S(1)} %get-tuple-element.65) | copy-start | bytes 1540
  147.1 17.8 %collective-permute-start.4 = (f32[180224]{0:T(1024)S(1)}, f32[180224]{0:T(1024)S(1)}, u32[]{:S(2)}, u32[]{:S(2)}) collective-permute-start(f32[180224]{0:T(1024)S(1)} %pad_maximum_fusion.2), channel_id=1, source_target_pairs={{8,0},{16,8},{24,16},{0,24},{9,1},{17,9},{25,17},{1,25},{10,2},{18... | collective-permute-start | bytes 2162696 | tf_op jit(solution)/shard_map/ppermute | solution.py:30
  150.8 30.6 %collective-permute-start.5 = (f32[180224]{0:T(1024)S(1)}, f32[180224]{0:T(1024)S(1)}, u32[]{:S(2)}, u32[]{:S(2)}) collective-permute-start(f32[180224]{0:T(1024)S(1)} %pad_maximum_fusion.3), channel_id=1, source_target_pairs={{24,0},{0,8},{8,16},{16,24},{25,1},{1,9},{9,17},{17,25},{26,2},{2,... | collective-permute-start | bytes 2162696 | tf_op jit(solution)/shard_map/ppermute | solution.py:30
  152.1 29.2 %collective-permute-start.6 = (f32[180224]{0:T(1024)S(1)}, f32[180224]{0:T(1024)S(1)}, u32[]{:S(2)}, u32[]{:S(2)}) collective-permute-start(f32[180224]{0:T(1024)S(1)} %pad_maximum_fusion.4), channel_id=1, source_target_pairs={{1,0},{2,1},{3,2},{4,3},{5,4},{6,5},{7,6},{0,7},{9,8},{10,9},{11,1... | collective-permute-start | bytes 2162696 | tf_op jit(solution)/shard_map/ppermute | solution.py:30
  153.8 27.5 %collective-permute-start.7 = (f32[180224]{0:T(1024)S(1)}, f32[180224]{0:T(1024)S(1)}, u32[]{:S(2)}, u32[]{:S(2)}) collective-permute-start(f32[180224]{0:T(1024)S(1)} %pad_maximum_fusion.5), channel_id=1, source_target_pairs={{7,0},{0,1},{1,2},{2,3},{3,4},{4,5},{5,6},{6,7},{15,8},{8,9},{9,10... | collective-permute-start | bytes 2162696 | tf_op jit(solution)/shard_map/ppermute | solution.py:30
  158.4 23.0 %copy-start.47 = (f32[2048,128]{1,0:T(8,128)S(1)}, f32[2048,128]{1,0:T(8,128)}, u32[]{:S(2)}) copy-start(f32[2048,128]{1,0:T(8,128)} %fusion.256) | copy-start | bytes 3145732
  158.4 23.0 %copy-start.87 = (f32[1,1,128,128]{3,2,1,0:T(8,128)S(1)}, f32[1,1,128,128]{3,2,1,0:T(8,128)}, u32[]{:S(2)}) copy-start(f32[1,1,128,128]{3,2,1,0:T(8,128)} %param.20) | copy-start | bytes 196612
  160.9 21.0 %copy-start.22 = (bf16[2048,128]{1,0:T(8,128)(2,1)S(1)}, bf16[2048,128]{1,0:T(8,128)(2,1)}, u32[]{:S(2)}) copy-start(bf16[2048,128]{1,0:T(8,128)(2,1)} %get-tuple-element.84) | copy-start | bytes 1572868
  160.9 21.0 %copy-start.27 = (bf16[2048,128]{1,0:T(8,128)(2,1)S(1)}, bf16[2048,128]{1,0:T(8,128)(2,1)}, u32[]{:S(2)}) copy-start(bf16[2048,128]{1,0:T(8,128)(2,1)} %fusion.30) | copy-start | bytes 1572868
  160.9 21.0 %copy-start.68 = (f32[1,1,128,128]{3,2,1,0:T(8,128)S(1)}, f32[1,1,128,128]{3,2,1,0:T(8,128)}, u32[]{:S(2)}) copy-start(f32[1,1,128,128]{3,2,1,0:T(8,128)} %param.17) | copy-start | bytes 196612
  160.9 23.3 %copy-start.21 = (f32[1,1,1024,128]{3,2,1,0:T(8,128)S(1)}, f32[1,1,1024,128]{3,2,1,0:T(8,128)}, u32[]{:S(2)}) copy-start(f32[1,1,1024,128]{3,2,1,0:T(8,128)} %param.18) | copy-start | bytes 1572868
  181.9 21.1 %copy-start.88 = (f32[128,128]{1,0:T(8,128)}, f32[128,128]{1,0:T(8,128)S(1)}, u32[]{:S(2)}) copy-start(f32[128,128]{1,0:T(8,128)S(1)} %fusion.183) | copy-start | bytes 196612
  181.9 19.2 %copy-start.106 = (bf16[2,128]{1,0:T(2,128)(2,1)S(1)}, bf16[2,128]{1,0:T(2,128)(2,1)}, u32[]{:S(2)}) copy-start(bf16[2,128]{1,0:T(2,128)(2,1)} %copy-done.105) | copy-start | bytes 1540
  198.6 17.6 %collective-permute-start.8 = (bf16[1,1,180480]{2,0,1:T(2,128)(2,1)S(1)}, bf16[1,1,180480]{2,0,1:T(2,128)(2,1)S(1)}, u32[]{:S(2)}, u32[]{:S(2)}) collective-permute-start(bf16[1,1,180480]{2,0,1:T(2,128)(2,1)S(1)} %broadcast_in_dim.37), channel_id=1, source_target_pairs={{0,8},{8,16},{16,24},{24,0},{1,9},{9,17},{17,25},{25,1},{2,10},{10... | collective-permute-start | bytes 1082888 | tf_op jit(solution)/shard_map/ppermute | solution.py:19
  199.8 30.7 %collective-permute-start.9 = (bf16[1,1,180480]{2,0,1:T(2,128)(2,1)S(1)}, bf16[1,1,180480]{2,0,1:T(2,128)(2,1)S(1)}, u32[]{:S(2)}, u32[]{:S(2)}) collective-permute-start(bf16[1,1,180480]{2,0,1:T(2,128)(2,1)S(1)} %broadcast_in_dim.37), channel_id=1, source_target_pairs={{8,0},{16,8},{24,16},{0,24},{9,1},{17,9},{25,17},{1,25},{10,2},{18... | collective-permute-start | bytes 1082888 | tf_op jit(solution)/shard_map/ppermute | solution.py:22
  233.0 34.3 %collective-permute-start.11 = (bf16[3,1,180480]{2,0,1:T(4,128)(2,1)S(1)}, bf16[3,1,180480]{2,0,1:T(4,128)(2,1)S(1)}, u32[]{:S(2)}, u32[]{:S(2)}) collective-permute-start(bf16[3,1,180480]{2,0,1:T(4,128)(2,1)S(1)} %pad_maximum_fusion.1), channel_id=1, source_target_pairs={{1,0},{2,1},{3,2},{4,3},{5,4},{6,5},{7,6},{0,7},{9,8},{10,9},{11,1... | collective-permute-start | bytes 3248648 | tf_op jit(solution)/shard_map/ppermute | solution.py:22
  234.9 35.3 %collective-permute-start.10 = (bf16[3,1,180480]{2,0,1:T(4,128)(2,1)S(1)}, bf16[3,1,180480]{2,0,1:T(4,128)(2,1)S(1)}, u32[]{:S(2)}, u32[]{:S(2)}) collective-permute-start(bf16[3,1,180480]{2,0,1:T(4,128)(2,1)S(1)} %pad_maximum_fusion.1), channel_id=1, source_target_pairs={{0,1},{1,2},{2,3},{3,4},{4,5},{5,6},{6,7},{7,0},{8,9},{9,10},{10,1... | collective-permute-start | bytes 3248648 | tf_op jit(solution)/shard_map/ppermute | solution.py:19
  333.7 18.0 %collective-permute-start.12 = (f32[180224]{0:T(1024)S(1)}, f32[180224]{0:T(1024)S(1)}, u32[]{:S(2)}, u32[]{:S(2)}) collective-permute-start(f32[180224]{0:T(1024)S(1)} %pad_maximum_fusion.6), channel_id=1, source_target_pairs={{8,0},{16,8},{24,16},{0,24},{9,1},{17,9},{25,17},{1,25},{10,2},{18... | collective-permute-start | bytes 2162696 | tf_op jit(solution)/shard_map/ppermute | solution.py:30
  337.2 30.9 %collective-permute-start.13 = (f32[180224]{0:T(1024)S(1)}, f32[180224]{0:T(1024)S(1)}, u32[]{:S(2)}, u32[]{:S(2)}) collective-permute-start(f32[180224]{0:T(1024)S(1)} %pad_maximum_fusion.7), channel_id=1, source_target_pairs={{24,0},{0,8},{8,16},{16,24},{25,1},{1,9},{9,17},{17,25},{26,2},{2,... | collective-permute-start | bytes 2162696 | tf_op jit(solution)/shard_map/ppermute | solution.py:30
  338.5 29.6 %collective-permute-start.14 = (f32[180224]{0:T(1024)S(1)}, f32[180224]{0:T(1024)S(1)}, u32[]{:S(2)}, u32[]{:S(2)}) collective-permute-start(f32[180224]{0:T(1024)S(1)} %pad_maximum_fusion.8), channel_id=1, source_target_pairs={{1,0},{2,1},{3,2},{4,3},{5,4},{6,5},{7,6},{0,7},{9,8},{10,9},{11,1... | collective-permute-start | bytes 2162696 | tf_op jit(solution)/shard_map/ppermute | solution.py:30
  339.9 28.2 %collective-permute-start.15 = (f32[180224]{0:T(1024)S(1)}, f32[180224]{0:T(1024)S(1)}, u32[]{:S(2)}, u32[]{:S(2)}) collective-permute-start(f32[180224]{0:T(1024)S(1)} %pad_maximum_fusion.9), channel_id=1, source_target_pairs={{7,0},{0,1},{1,2},{2,3},{3,4},{4,5},{5,6},{6,7},{15,8},{8,9},{9,10... | collective-permute-start | bytes 2162696 | tf_op jit(solution)/shard_map/ppermute | solution.py:30
  343.0 25.1 %copy-start.50 = (f32[2048,128]{1,0:T(8,128)S(1)}, f32[2048,128]{1,0:T(8,128)}, u32[]{:S(2)}) copy-start(f32[2048,128]{1,0:T(8,128)} %copy-done.48) | copy-start | bytes 3145732
  343.0 25.1 %copy-start.90 = (f32[128,128]{1,0:T(8,128)S(1)}, f32[128,128]{1,0:T(8,128)}, u32[]{:S(2)}) copy-start(f32[128,128]{1,0:T(8,128)} %copy-done.88) | copy-start | bytes 196612
  345.5 23.7 %copy-start.5 = (f32[1024,128]{1,0:T(8,128)S(1)}, f32[1024,128]{1,0:T(8,128)}, u32[]{:S(2)}) copy-start(f32[1024,128]{1,0:T(8,128)} %copy-done.4) | copy-start | bytes 1572868
  345.5 24.7 %copy-start.3 = (bf16[2048,128]{1,0:T(8,128)(2,1)S(1)}, bf16[2048,128]{1,0:T(8,128)(2,1)}, u32[]{:S(2)}) copy-start(bf16[2048,128]{1,0:T(8,128)(2,1)} %copy-done.2) | copy-start | bytes 1572868
  (123 other events, 502.1 us)
where the time goes:
time: 379 us; the launch traced here: 371 us
  waiting for transfers between devices  123 us (32%)
  matrix products  115 us (30%)
  other arithmetic  63 us (17%)
  local copies, waits for them, and re-layouts  46.6 us (12%)
  starting transfers between devices  21.3 us (6%)
    dot_general x58, matrix products, matmul(): return jnp.dot(left_side, right_side, preferred_element_type=jnp.float32)  76.1 us
    ppermute x4, waiting for transfers between devices, padded(): lax.ppermute(lax.slice_in_dim(block, 0, width, axis=dim), axis, backward)  51.7 us
    ppermute x8, waiting for transfers between devices, shifted_2(): return lax.ppermute(block, axis, route)  43 us
    dot_general x24, matrix products, rows_matmul(): lax.dot_general(left_side, right_side, (((0,), (0,)), ((), ())), preferre...  36.4 us
    ppermute x4, waiting for transfers between devices, padded(): lax.ppermute(lax.slice_in_dim(block, block.shape[dim] - width, None, axis...  27.9 us
    reduce_sum x2, other arithmetic, on_device(): grad_out = jnp.sum(disc_stored[3] * weight_rows[:, None], axis=0)  17.1 us
    unnamed x286, local copies, waits for them, and re-layouts  16.6 us
    mul x10, other arithmetic, silu_slope(): return sigmoid_part * (1.0 + values * (1.0 - sigmoid_part))  14.5 us
  transfers between devices with their start and end apart: 16, of which 10 were waited for; matrix products, arithmetic and copies ran while one was open for 16% of the time, Pallas kernels for 0%

commit v1 on v0

v1 whole, which is shorter than its diff:
```python
import functools

import jax
import jax.numpy as jnp
from jax import lax
from jax.experimental import pallas as pl
from jax.experimental.pallas import tpu as pltpu
from jax.sharding import PartitionSpec as P

learn_rate = 0.05
base_rate = 0.1

TILE = 256
MESH = pl.DeviceIdType.MESH
f32 = jnp.float32
bf16 = jnp.bfloat16


def dot(left, right):
    return jnp.dot(left, right, preferred_element_type=f32)


def rows_dot(left, right):
    return lax.dot_general(left, right, (((0,), (0,)), ((), ())), preferred_element_type=f32)


def sigmoid(values):
    return 0.5 + 0.5 * jnp.tanh(0.5 * values)


def silu_parts(values):
    gate = sigmoid(values)
    act = values * gate
    return act, gate + act * (1.0 - gate)


def pair_lanes(left, right):
    return jnp.concatenate([left, right], axis=1)


def put_blocks(ref, weights):
    size = weights.shape[0]
    nothing = jnp.zeros((size, size), bf16)
    ref[...] = jnp.concatenate(
        [pair_lanes(weights, nothing), pair_lanes(nothing, weights)], axis=0
    )


def half_sum(blocks, scale):
    size = blocks.shape[0] // 2
    return (
        blocks[:size, :size] * scale[:, :size] + blocks[size:, size:] * scale[:, size:]
    )


def opposite(way):
    return way + 1 - 2 * lax.rem(way, 2)


def train_kernel(
    rows_count,
    cols_count,
    steps,
    reals_ref, seed_ref, bank_ref,
    g_in_ref, g_base_ref, g_one_ref, g_two_ref, d_one_ref, d_two_ref, d_out_ref,
    n_in, n_base, n_one, n_two, n_done, n_dtwo, n_dout, verdict_ref,
    small_own, base_own, small_in, base_in,
    cot_own, cot_out, cot_in, scale_own, scale_out, scale_in,
    hidden_s, middle_s, slope_pre_s, slope_mid_s,
    one_b, two_b, one_tb, two_tb, own_one_tb, own_two_tb,
    d1_b, d2_b, d1_tb, d2_tb,
    acc_one, acc_two, acc_feat, sum_done, sum_dtwo, sum_dout,
    latent_s,
    fwd_send, fwd_recv, ret_send, ret_recv, sc_send, sc_recv,
):
    places, channels = g_base_ref.shape
    tiles = places // TILE
    my_row = lax.axis_index("row")
    my_col = lax.axis_index("col")

    def device_of(way):
        along = 2 * lax.rem(way, 2) - 1
        vertical = 1 - way // 2
        row = lax.rem(my_row + along * vertical + rows_count, rows_count)
        col = lax.rem(my_col + along * (1 - vertical) + cols_count, cols_count)
        return (row, col)

    def rows_of(tile):
        return pl.ds(pl.multiple_of(tile * TILE, TILE), TILE)

    def small_copy(step, way, slot):
        return pltpu.make_async_remote_copy(
            src_ref=small_own, dst_ref=small_in.at[step, slot],
            send_sem=fwd_send.at[step, way, 0], recv_sem=fwd_recv.at[step, slot, 0],
            device_id=device_of(way), device_id_type=MESH,
        )

    def base_copy(step, way, slot, tile):
        return pltpu.make_async_remote_copy(
            src_ref=base_own.at[rows_of(tile)], dst_ref=base_in.at[step, slot, rows_of(tile)],
            send_sem=fwd_send.at[step, way, tile + 1], recv_sem=fwd_recv.at[step, slot, tile + 1],
            device_id=device_of(way), device_id_type=MESH,
        )

    def cot_copy(step, way, slot, tile):
        return pltpu.make_async_remote_copy(
            src_ref=cot_out.at[step, way, rows_of(tile)],
            dst_ref=cot_in.at[step, slot, rows_of(tile)],
            send_sem=ret_send.at[step, way, tile], recv_sem=ret_recv.at[step, slot, tile],
            device_id=device_of(way), device_id_type=MESH,
        )

    def scale_copy(step, way, slot):
        return pltpu.make_async_remote_copy(
            src_ref=scale_out.at[step, way], dst_ref=scale_in.at[step, slot],
            send_sem=sc_send.at[step, way], recv_sem=sc_recv.at[step, slot],
            device_id=device_of(way), device_id_type=MESH,
        )

    barrier = pltpu.get_barrier_semaphore()
    for way in range(4):
        pl.semaphore_signal(barrier, inc=1, device_id=device_of(way), device_id_type=MESH)

    n_in[...] = g_in_ref[...]
    n_base[...] = g_base_ref[...]
    n_one[...] = g_one_ref[...]
    n_two[...] = g_two_ref[...]
    n_done[...] = d_one_ref[...]
    n_dtwo[...] = d_two_ref[...]
    n_dout[...] = d_out_ref[...]
    bank_rows = bank_ref.shape[0]
    chosen = seed_ref[...] == lax.broadcasted_iota(jnp.int32, (seed_ref.shape[0], bank_rows), 1)
    latent_s[...] = dot(chosen.astype(f32).astype(bf16), bank_ref[...].astype(bf16)).reshape(
        latent_s.shape
    )
    verdict_ref[...] = jnp.zeros_like(verdict_ref)
    pl.semaphore_wait(barrier, 4)

    def shifts_of(small):
        hi = small[2 * channels : 2 * channels + 16].astype(f32)
        return hi[0:1] + hi[2:3] + hi[4:5], hi[1:2] + hi[3:4] + hi[5:6]

    def made(base, shift_a, shift_b, one, two, keep):
        base = base.astype(f32)
        gen_pre = pair_lanes(base + shift_a, base + shift_b)
        act, slope = silu_parts(gen_pre)
        hidden = act.astype(bf16)
        middle_pre = dot(hidden, one)
        act_mid, slope_mid = silu_parts(middle_pre)
        middle = act_mid.astype(bf16)
        if keep is not None:
            hidden_s[keep] = hidden
            middle_s[keep] = middle
            slope_pre_s[keep] = slope
            slope_mid_s[keep] = slope_mid
        return (hidden.astype(f32) + dot(middle, two)).astype(bf16)

    def judge_tile(images, d_out_pair):
        first_pre = dot(images, d1_b[...])
        act, slope_first = silu_parts(first_pre)
        first = act.astype(bf16)
        summed = images.astype(f32) + dot(first, d2_b[...])
        feature, slope_sum = silu_parts(summed)
        acc_feat[...] += jnp.sum(feature, axis=0, keepdims=True)
        outer = slope_sum * d_out_pair
        outer_half = outer.astype(bf16)
        inner = (dot(outer_half, d2_tb[...]) * slope_first).astype(bf16)
        acc_two[...] += rows_dot(first, outer_half)
        acc_one[...] += rows_dot(images, inner)
        return outer, inner

    def clear():
        acc_feat[...] = jnp.zeros_like(acc_feat)
        acc_one[...] = jnp.zeros_like(acc_one)
        acc_two[...] = jnp.zeros_like(acc_two)

    def settle(step, place, real):
        feats = acc_feat[...]
        weighted = feats * pair_lanes(n_dout[...], n_dout[...])
        shape = (1, channels)
        low = jnp.sum(weighted[:, :channels], axis=1, keepdims=True) * (1.0 / places)
        high = jnp.sum(weighted[:, channels:], axis=1, keepdims=True) * (1.0 / places)
        low = jnp.broadcast_to(low, shape)
        high = jnp.broadcast_to(high, shape)
        verdict_ref[step, place] = jnp.concatenate(
            [low, high, jnp.zeros((6, channels), f32)], axis=0
        )
        verdict = pair_lanes(low, high)
        against = -sigmoid(-verdict) * (1.0 / places)
        toward = against if real else sigmoid(verdict) * (1.0 / places)
        sum_done[...] += half_sum(acc_one[...], toward)
        sum_dtwo[...] += half_sum(acc_two[...], toward)
        scaled = feats * toward
        sum_dout[...] += scaled[:, :channels] + scaled[:, channels:]
        return jnp.broadcast_to(against, (8, 2 * channels))

    def one_step(step, carry):
        base_own[...] = n_base[...].astype(bf16)
        latent = latent_s[step].astype(bf16)
        shift = dot(latent, n_in[...].astype(bf16))
        top = shift.astype(bf16)
        rest = shift - top.astype(f32)
        mid = rest.astype(bf16)
        last = rest - mid.astype(f32)
        small_own[0:channels] = n_one[...].astype(bf16)
        small_own[channels : 2 * channels] = n_two[...].astype(bf16)
        small_own[2 * channels : 2 * channels + 16] = jnp.concatenate(
            [top[0:2].astype(f32), mid[0:2].astype(f32), last[0:2], jnp.zeros((10, channels), f32)],
            axis=0,
        ).astype(bf16)

        def send_ways(way, carry):
            small_copy(step, way, opposite(way)).start()
            return carry

        def send_bases(at, carry):
            way = lax.rem(at, 4)
            base_copy(step, way, opposite(way), at // 4).start()
            return carry

        lax.fori_loop(0, 4, send_ways, 0)
        lax.fori_loop(0, 4 * tiles, send_bases, 0)

        put_blocks(one_b, n_one[...].astype(bf16))
        put_blocks(two_b, n_two[...].astype(bf16))
        put_blocks(own_one_tb, n_one[...].T.astype(bf16))
        put_blocks(own_two_tb, n_two[...].T.astype(bf16))
        put_blocks(d1_b, n_done[...].astype(bf16))
        put_blocks(d2_b, n_dtwo[...].astype(bf16))
        put_blocks(d1_tb, n_done[...].T.astype(bf16))
        put_blocks(d2_tb, n_dtwo[...].T.astype(bf16))
        sum_done[...] = jnp.zeros_like(sum_done)
        sum_dtwo[...] = jnp.zeros_like(sum_dtwo)
        sum_dout[...] = jnp.zeros_like(sum_dout)
        d_out_pair = pair_lanes(n_dout[...], n_dout[...])

        clear()

        def own_tile(tile, carry):
            at = rows_of(tile)
            images = made(base_own[at], shift[0:1], shift[1:2], one_b[...], two_b[...], at)
            outer, inner = judge_tile(images, d_out_pair)
            cot_own[at] = (outer + dot(inner, d1_tb[...])).astype(bf16)
            return carry

        lax.fori_loop(0, tiles, own_tile, 0)
        scale_own[...] = settle(step, 0, False)

        clear()

        def real_tile(tile, carry):
            at = rows_of(tile)
            judge_tile(pair_lanes(reals_ref[2 * step, at], reals_ref[2 * step + 1, at]), d_out_pair)
            return carry

        lax.fori_loop(0, tiles, real_tile, 0)
        settle(step, 5, True)

        def beside(order, carry):
            way = 3 - order
            small_copy(step, way, way).wait_recv()
            small = small_in.at[step, way]
            put_blocks(one_b, small[0:channels])
            put_blocks(two_b, small[channels : 2 * channels])
            shift_a, shift_b = shifts_of(small)
            clear()

            def their_tile(tile, carry):
                at = rows_of(tile)
                base_copy(step, way, way, tile).wait_recv()
                images = made(base_in[step, way, at], shift_a, shift_b, one_b[...], two_b[...], None)
                outer, inner = judge_tile(images, d_out_pair)
                cot_out[step, way, at] = (outer + dot(inner, d1_tb[...])).astype(bf16)
                cot_copy(step, way, opposite(way), tile).start()
                return carry

            lax.fori_loop(0, tiles, their_tile, 0)
            scale_out[step, way] = settle(step, way + 1, False)
            scale_copy(step, way, opposite(way)).start()
            return carry

        lax.fori_loop(0, 4, beside, 0)

        n_done[...] -= learn_rate * sum_done[...]
        n_dtwo[...] -= learn_rate * sum_dtwo[...]
        n_dout[...] -= learn_rate * sum_dout[...]

        clear()

        def scale_waits(way, carry):
            scale_copy(step, way, way).wait_recv()
            return carry

        lax.fori_loop(0, 4, scale_waits, 0)

        def back_tile(tile, carry):
            at = rows_of(tile)

            def cot_waits(way, carry):
                cot_copy(step, way, way, tile).wait_recv()
                return carry

            lax.fori_loop(0, 4, cot_waits, 0)
            total = cot_own[at].astype(f32) * scale_own[0:1]
            for way in range(4):
                total += cot_in[step, way, at].astype(f32) * scale_in[step, way, 0:1]
            half = total.astype(bf16)
            acc_two[...] += rows_dot(middle_s[at], half)
            inner = (dot(half, own_two_tb[...]) * slope_mid_s[at]).astype(bf16)
            acc_one[...] += rows_dot(hidden_s[at], inner)
            outer = (total + dot(inner, own_one_tb[...])) * slope_pre_s[at]
            acc_feat[...] += jnp.sum(outer, axis=0, keepdims=True)
            n_base[at] -= (base_rate * places) * (outer[:, :channels] + outer[:, channels:])
            return carry

        lax.fori_loop(0, tiles, back_tile, 0)
        n_one[...] -= learn_rate * (
            acc_one[:channels, :channels] + acc_one[channels:, channels:]
        )
        n_two[...] -= learn_rate * (
            acc_two[:channels, :channels] + acc_two[channels:, channels:]
        )
        sums = acc_feat[...]
        sums = jnp.concatenate(
            [sums[:, :channels], sums[:, channels:], jnp.zeros((6, channels), f32)], axis=0
        )
        n_in[...] -= learn_rate * lax.dot_general(
            latent_s[step], sums, (((0,), (0,)), ((), ())),
            precision=lax.Precision.HIGHEST, preferred_element_type=f32,
        )

        def sent(way, carry):
            small_copy(step, way, way).wait_send()
            scale_copy(step, way, way).wait_send()

            def sent_tile(tile, carry):
                base_copy(step, way, way, tile).wait_send()
                cot_copy(step, way, way, tile).wait_send()
                return carry

            return lax.fori_loop(0, tiles, sent_tile, carry)

        lax.fori_loop(0, 4, sent, 0)
        return carry

    lax.fori_loop(0, steps, one_step, 0)


def pick_kernel(index_ref, data_ref, out_ref):
    out_ref[...] = data_ref[...]


def pick(data, index):
    count = index.shape[0]
    block = (1,) + data.shape[1:]
    return pl.pallas_call(
        pick_kernel,
        out_shape=jax.ShapeDtypeStruct((count,) + data.shape[1:], data.dtype),
        grid_spec=pltpu.PrefetchScalarGridSpec(
            num_scalar_prefetch=1,
            grid=(count,),
            in_specs=[pl.BlockSpec(block, lambda i, index_ref: (index_ref[i], 0, 0))],
            out_specs=pl.BlockSpec(block, lambda i, index_ref: (i, 0, 0)),
        ),
    )(index, data)


def on_device(
    rows_count, cols_count,
    data, real_index, latent_seed, latent_bank, g_in, g_base, g_one, g_two, d_one, d_two, d_out,
):
    steps = real_index.shape[2]
    places, channels = data.shape[3:]
    reals = pick(data[0, 0], real_index.reshape(-1))
    seed = latent_seed.reshape(steps, 2)
    seed = jnp.concatenate([seed, jnp.full((steps, 6), -1, jnp.int32)], axis=1).reshape(-1, 1)
    wide = 2 * channels
    square = (channels, channels)
    blocks = pltpu.VMEM((wide, wide), bf16)
    tiles = places // TILE
    vmem = pl.BlockSpec(memory_space=pltpu.VMEM)
    small = 2 * channels + 16
    shapes = [square, (places, channels), square, square, square, square, (1, channels)]
    outs = pl.pallas_call(
        functools.partial(train_kernel, rows_count, cols_count, steps),
        out_shape=[jax.ShapeDtypeStruct(shape, f32) for shape in shapes]
        + [jax.ShapeDtypeStruct((steps, 6, 8, channels), f32)],
        in_specs=[vmem] * 10,
        out_specs=[vmem] * 8,
        scratch_shapes=[
            pltpu.VMEM((small, channels), bf16),
            pltpu.VMEM((places, channels), bf16),
            pltpu.VMEM((steps, 4, small, channels), bf16),
            pltpu.VMEM((steps, 4, places, channels), bf16),
            pltpu.VMEM((places, wide), bf16),
            pltpu.VMEM((steps, 4, places, wide), bf16),
            pltpu.VMEM((steps, 4, places, wide), bf16),
            pltpu.VMEM((8, wide), f32),
            pltpu.VMEM((steps, 4, 8, wide), f32),
            pltpu.VMEM((steps, 4, 8, wide), f32),
            pltpu.VMEM((places, wide), bf16),
            pltpu.VMEM((places, wide), bf16),
            pltpu.VMEM((places, wide), f32),
            pltpu.VMEM((places, wide), f32),
        ]
        + [blocks] * 10
        + [
            pltpu.VMEM((wide, wide), f32),
            pltpu.VMEM((wide, wide), f32),
            pltpu.VMEM((1, wide), f32),
            pltpu.VMEM(square, f32),
            pltpu.VMEM(square, f32),
            pltpu.VMEM((1, channels), f32),
            pltpu.VMEM((steps, 8, channels), f32),
            pltpu.SemaphoreType.DMA((steps, 4, tiles + 1)),
            pltpu.SemaphoreType.DMA((steps, 4, tiles + 1)),
            pltpu.SemaphoreType.DMA((steps, 4, tiles)),
            pltpu.SemaphoreType.DMA((steps, 4, tiles)),
            pltpu.SemaphoreType.DMA((steps, 4)),
            pltpu.SemaphoreType.DMA((steps, 4)),
        ],
        compiler_params=pltpu.CompilerParams(
            collective_id=0, has_side_effects=True, vmem_limit_bytes=50 * 1024 * 1024
        ),
    )(
        reals, seed, latent_bank,
        g_in[0, 0], g_base[0, 0], g_one[0, 0], g_two[0, 0], d_one[0, 0], d_two[0, 0],
        d_out.reshape(1, channels),
    )
    verdicts = outs[7][:, :, :2, 0].reshape(1, 1, steps, 12)
    finals = [member[None, None] for member in outs[:6]] + [outs[6].reshape(1, 1, channels)]
    return (*finals, verdicts)


def solution(mesh):
    whole = P("row", "col", None, None)
    return jax.shard_map(
        functools.partial(on_device, mesh.shape["row"], mesh.shape["col"]),
        mesh=mesh,
        in_specs=(P("row", "col", None, None, None), whole, whole, P()) + (whole,) * 6
        + (P("row", "col", None),),
        out_specs=(whole,) * 6 + (P("row", "col", None), whole),
        check_vma=False,
    )
```

time: 379 us -> 106 us (0.28)
  the two profiles are of different devices: /device:TPU:13 before, /device:TPU:0 now
where the time goes in v1:
time: 106 us
  Pallas kernels  96.9 us (91%)
  local copies, waits for them, and re-layouts  8.55 us (8%)
    pallas_call x1, Pallas kernels, on_device(): pl.pallas_call(functools.partial(train_kernel, rows_count, cols_count, st...  92.9 us
    unnamed x25, local copies, waits for them, and re-layouts  5.7 us
    pallas_call x1, Pallas kernels, pick(): pl.pallas_call(pick_kernel, out_shape=jax.ShapeDtypeStruct((count,) + dat...  4.03 us

profile of v1, /device:TPU:0, one launch (start us, length us, event | category | flops | bytes accessed | tf_op | source)
XLA Modules:
  0.0 106.2 jit_solution(8659591691229457524)
XLA Ops:
  0.6 0.0 copy-start.8
  0.6 0.0 copy-start.7
  0.7 0.0 copy-start.6
  0.7 0.0 copy-start.5
  0.7 0.0 copy-start.4
  0.7 0.0 copy-start.1
  0.7 0.0 copy-start.3
  0.7 0.0 copy-start.2
  0.7 1.4 %reshape.31.index_ref = s32[4]{0:T(128)} reshape(s32[1,1,2,2]{3,2,1,0:T(2,128)} %param.12) | data formatting | bytes 32 | tf_op jit(solution)/shard_map/reshape | solution.py:374
  2.1 0.7 concatenate.3
  2.8 0.1 reshape.36.seed_ref
  2.8 4.0 %shard_map.170.reals_ref = bf16[4,1024,128]{2,1,0:T(8,128)(2,1)} custom-call(s32[4]{0:T(128)} %reshape.31.index_ref, bf16[32,1024,128]{2,1,0:T(8,128)(2,1)} %bitcast.30), custom_call_target="tpu_custom_call" | custom-call | tf_op jit(solution)/shard_map/pallas_call | solution.py:356
  6.9 0.0 copy-done.8
  6.9 0.0 copy-done.7
  6.9 0.0 copy-done.6
  6.9 0.0 copy-done.5
  6.9 0.0 copy-done.4
  6.9 0.0 copy-done.1
  6.9 0.0 copy-done.3
  6.9 0.0 copy-done.2
  6.9 0.0 copy-start
  6.9 1.2 %copy-done = bf16[4,1024,128]{2,1,0:T(8,128)(2,1)S(1)} copy-done((bf16[4,1024,128]{2,1,0:T(8,128)(2,1)S(1)}, bf16[4,1024,128]{2,1,0:T(8,128)(2,1)}, u32[]{:S(2)}) %copy-start) | copy-done | bytes 1048600
  8.1 92.9 %shard_map.171 = (f32[128,128]{1,0:T(8,128)S(1)}, f32[1024,128]{1,0:T(8,128)S(1)}, f32[128,128]{1,0:T(8,128)S(1)}, f32[128,128]{1,0:T(8,128)S(1)}, f32[128,128]{...) custom-call(bf16[4,1024,128]{2,1,0:T(8,128)(2,1)S(1)} %copy-done, ...), custom_call_target="tpu_custom_call" | custom-call | tf_op jit(solution)/shard_map/pallas_call | solution.py:384
  101.0 0.1 slice_reduce_fusion
  101.1 0.7 reshape_squeeze.3
  101.8 0.6 copy.28
  102.4 0.8 copy.29
  103.2 0.6 copy.30
  103.8 0.6 copy.31
  104.5 0.6 copy.32
  105.1 0.6 copy.33
  105.7 0.5 copy.34
Async XLA Ops:
  0.6 6.2 %copy-start.8 = (f32[1,1,128]{2,1,0:T(1,128)S(1)}, f32[1,1,128]{2,1,0:T(1,128)}, u32[]{:S(2)}) copy-start(f32[1,1,128]{2,1,0:T(1,128)} %param.21) | copy-start | bytes 1540
  0.6 6.2 %copy-start.7 = (f32[1,1,128,128]{3,2,1,0:T(8,128)S(1)}, f32[1,1,128,128]{3,2,1,0:T(8,128)}, u32[]{:S(2)}) copy-start(f32[1,1,128,128]{3,2,1,0:T(8,128)} %param.20) | copy-start | bytes 196612
  0.7 6.2 %copy-start.6 = (f32[1,1,128,128]{3,2,1,0:T(8,128)S(1)}, f32[1,1,128,128]{3,2,1,0:T(8,128)}, u32[]{:S(2)}) copy-start(f32[1,1,128,128]{3,2,1,0:T(8,128)} %param.19) | copy-start | bytes 196612
  0.7 6.2 %copy-start.5 = (f32[1,1,128,128]{3,2,1,0:T(8,128)S(1)}, f32[1,1,128,128]{3,2,1,0:T(8,128)}, u32[]{:S(2)}) copy-start(f32[1,1,128,128]{3,2,1,0:T(8,128)} %param.18) | copy-start | bytes 196612
  0.7 6.2 %copy-start.4 = (f32[1,1,128,128]{3,2,1,0:T(8,128)S(1)}, f32[1,1,128,128]{3,2,1,0:T(8,128)}, u32[]{:S(2)}) copy-start(f32[1,1,128,128]{3,2,1,0:T(8,128)} %param.17) | copy-start | bytes 196612
  0.7 6.2 %copy-start.1 = (f32[1,1,1024,128]{3,2,1,0:T(8,128)S(1)}, f32[1,1,1024,128]{3,2,1,0:T(8,128)}, u32[]{:S(2)}) copy-start(f32[1,1,1024,128]{3,2,1,0:T(8,128)} %param.16) | copy-start | bytes 1572868
  0.7 6.2 %copy-start.3 = (f32[1,1,128,128]{3,2,1,0:T(8,128)S(1)}, f32[1,1,128,128]{3,2,1,0:T(8,128)}, u32[]{:S(2)}) copy-start(f32[1,1,128,128]{3,2,1,0:T(8,128)} %param.15) | copy-start | bytes 196612
  0.7 6.2 %copy-start.2 = (f32[256,128]{1,0:T(8,128)S(1)}, f32[256,128]{1,0:T(8,128)}, u32[]{:S(2)}) copy-start(f32[256,128]{1,0:T(8,128)} %bank_ref.1) | copy-start | bytes 393220
  6.9 1.2 %copy-start = (bf16[4,1024,128]{2,1,0:T(8,128)(2,1)S(1)}, bf16[4,1024,128]{2,1,0:T(8,128)(2,1)}, u32[]{:S(2)}) copy-start(bf16[4,1024,128]{2,1,0:T(8,128)(2,1)} %shard_map.170.reals_ref) | copy-start | bytes 3145732

commit v2 on v1

--- a/solution.py
+++ b/solution.py
@@ -10,7 +10,7 @@
 learn_rate = 0.05
 base_rate = 0.1
 
-TILE = 256
+TILE = 512
 MESH = pl.DeviceIdType.MESH
 f32 = jnp.float32
 bf16 = jnp.bfloat16
@@ -29,9 +29,10 @@
 
 
 def silu_parts(values):
-    gate = sigmoid(values)
-    act = values * gate
-    return act, gate + act * (1.0 - gate)
+    half = 0.5 * values
+    twice = 1.0 + jnp.tanh(half)
+    act = half * twice
+    return act, twice * ((1.0 + values) - act)
 
 
 def pair_lanes(left, right):
@@ -61,7 +62,7 @@
     rows_count,
     cols_count,
     steps,
-    reals_ref, seed_ref, bank_ref,
+    reals_hbm, seed_ref, bank_ref,
     g_in_ref, g_base_ref, g_one_ref, g_two_ref, d_one_ref, d_two_ref, d_out_ref,
     n_in, n_base, n_one, n_two, n_done, n_dtwo, n_dout, verdict_ref,
     small_own, base_own, small_in, base_in,
@@ -70,7 +71,7 @@
     one_b, two_b, one_tb, two_tb, own_one_tb, own_two_tb,
     d1_b, d2_b, d1_tb, d2_tb,
     acc_one, acc_two, acc_feat, sum_done, sum_dtwo, sum_dout,
-    latent_s,
+    latent_s, reals_ref, real_sem,
     fwd_send, fwd_recv, ret_send, ret_recv, sc_send, sc_recv,
 ):
     places, channels = g_base_ref.shape
@@ -117,10 +118,16 @@
             device_id=device_of(way), device_id_type=MESH,
         )
 
+    def real_copy(step):
+        pair = pl.ds(2 * step, 2)
+        return pltpu.make_async_copy(reals_hbm.at[pair], reals_ref.at[pair], real_sem.at[step])
+
     barrier = pltpu.get_barrier_semaphore()
     for way in range(4):
         pl.semaphore_signal(barrier, inc=1, device_id=device_of(way), device_id_type=MESH)
 
+    for step in range(steps):
+        real_copy(step).start()
     n_in[...] = g_in_ref[...]
     n_base[...] = g_base_ref[...]
     n_one[...] = g_one_ref[...]
@@ -129,10 +136,13 @@
     n_dtwo[...] = d_two_ref[...]
     n_dout[...] = d_out_ref[...]
     bank_rows = bank_ref.shape[0]
-    chosen = seed_ref[...] == lax.broadcasted_iota(jnp.int32, (seed_ref.shape[0], bank_rows), 1)
-    latent_s[...] = dot(chosen.astype(f32).astype(bf16), bank_ref[...].astype(bf16)).reshape(
-        latent_s.shape
-    )
+    bank_half = bank_ref[...].astype(bf16)
+    at_row = lax.broadcasted_iota(jnp.int32, (8, bank_rows), 0)
+    at_lane = lax.broadcasted_iota(jnp.int32, (8, bank_rows), 1)
+    for step in range(steps):
+        wanted = jnp.where(at_row == 0, seed_ref[step, 0], seed_ref[step, 1])
+        chosen = jnp.where((wanted == at_lane) & (at_row < 2), 1.0, 0.0)
+        latent_s[step] = dot(chosen.astype(bf16), bank_half)
     verdict_ref[...] = jnp.zeros_like(verdict_ref)
     pl.semaphore_wait(barrier, 4)
 
@@ -224,15 +234,15 @@
         put_blocks(one_b, n_one[...].astype(bf16))
         put_blocks(two_b, n_two[...].astype(bf16))
         put_blocks(own_one_tb, n_one[...].T.astype(bf16))
-        put_blocks(own_two_tb, n_two[...].T.astype(bf16))
+        put_blocks(own_two_tb, (0.5 * n_two[...].T).astype(bf16))
         put_blocks(d1_b, n_done[...].astype(bf16))
         put_blocks(d2_b, n_dtwo[...].astype(bf16))
         put_blocks(d1_tb, n_done[...].T.astype(bf16))
-        put_blocks(d2_tb, n_dtwo[...].T.astype(bf16))
+        put_blocks(d2_tb, (0.5 * n_dtwo[...].T).astype(bf16))
         sum_done[...] = jnp.zeros_like(sum_done)
         sum_dtwo[...] = jnp.zeros_like(sum_dtwo)
         sum_dout[...] = jnp.zeros_like(sum_dout)
-        d_out_pair = pair_lanes(n_dout[...], n_dout[...])
+        d_out_pair = 0.5 * pair_lanes(n_dout[...], n_dout[...])
 
         clear()
 
@@ -247,6 +257,7 @@
         scale_own[...] = settle(step, 0, False)
 
         clear()
+        real_copy(step).wait()
 
         def real_tile(tile, carry):
             at = rows_of(tile)
@@ -310,7 +321,7 @@
             acc_one[...] += rows_dot(hidden_s[at], inner)
             outer = (total + dot(inner, own_one_tb[...])) * slope_pre_s[at]
             acc_feat[...] += jnp.sum(outer, axis=0, keepdims=True)
-            n_base[at] -= (base_rate * places) * (outer[:, :channels] + outer[:, channels:])
+            n_base[at] -= (0.5 * base_rate * places) * (outer[:, :channels] + outer[:, channels:])
             return carry
 
         lax.fori_loop(0, tiles, back_tile, 0)
@@ -324,7 +335,7 @@
         sums = jnp.concatenate(
             [sums[:, :channels], sums[:, channels:], jnp.zeros((6, channels), f32)], axis=0
         )
-        n_in[...] -= learn_rate * lax.dot_general(
+        n_in[...] -= (0.5 * learn_rate) * lax.dot_general(
             latent_s[step], sums, (((0,), (0,)), ((), ())),
             precision=lax.Precision.HIGHEST, preferred_element_type=f32,
         )
@@ -346,23 +357,54 @@
     lax.fori_loop(0, steps, one_step, 0)
 
 
-def pick_kernel(index_ref, data_ref, out_ref):
-    out_ref[...] = data_ref[...]
+def pick_kernel(index_ref, data_ref, out_ref, sem):
+    steps, count = index_ref.shape
+    copies = [
+        pltpu.make_async_copy(
+            data_ref.at[index_ref[i // count, i % count]], out_ref.at[i], sem.at[i]
+        )
+        for i in range(steps * count)
+    ]
+    for copy in copies:
+        copy.start()
+    for copy in copies:
+        copy.wait()
 
 
 def pick(data, index):
-    count = index.shape[0]
-    block = (1,) + data.shape[1:]
+    count = index.size
     return pl.pallas_call(
         pick_kernel,
         out_shape=jax.ShapeDtypeStruct((count,) + data.shape[1:], data.dtype),
-        grid_spec=pltpu.PrefetchScalarGridSpec(
-            num_scalar_prefetch=1,
-            grid=(count,),
-            in_specs=[pl.BlockSpec(block, lambda i, index_ref: (index_ref[i], 0, 0))],
-            out_specs=pl.BlockSpec(block, lambda i, index_ref: (i, 0, 0)),
-        ),
+        in_specs=[
+            pl.BlockSpec(memory_space=pltpu.SMEM), pl.BlockSpec(memory_space=pl.ANY)
+        ],
+        out_specs=pl.BlockSpec(memory_space=pl.ANY),
+        scratch_shapes=[pltpu.SemaphoreType.DMA((count,))],
+        compiler_params=pltpu.CompilerParams(vmem_limit_bytes=58 * 1024 * 1024),
     )(index, data)
+
+
+def hand_over_kernel(count, *refs):
+    copies = [
+        pltpu.make_async_copy(refs[i], refs[count + i], refs[-1].at[i]) for i in range(count)
+    ]
+    for copy in copies:
+        copy.start()
+    for copy in copies:
+        copy.wait()
+
+
+def hand_over(members):
+    count = len(members)
+    anywhere = pl.BlockSpec(memory_space=pl.ANY)
+    return pl.pallas_call(
+        functools.partial(hand_over_kernel, count),
+        out_shape=[jax.ShapeDtypeStruct(member.shape, member.dtype) for member in members],
+        in_specs=[anywhere] * count,
+        out_specs=[anywhere] * count,
+        scratch_shapes=[pltpu.SemaphoreType.DMA((count,))],
+    )(*members)
 
 
 def on_device(
@@ -371,9 +413,7 @@
 ):
     steps = real_index.shape[2]
     places, channels = data.shape[3:]
-    reals = pick(data[0, 0], real_index.reshape(-1))
-    seed = latent_seed.reshape(steps, 2)
-    seed = jnp.concatenate([seed, jnp.full((steps, 6), -1, jnp.int32)], axis=1).reshape(-1, 1)
+    reals = pick(data[0, 0], real_index[0, 0])
     wide = 2 * channels
     square = (channels, channels)
     blocks = pltpu.VMEM((wide, wide), bf16)
@@ -385,7 +425,8 @@
         functools.partial(train_kernel, rows_count, cols_count, steps),
         out_shape=[jax.ShapeDtypeStruct(shape, f32) for shape in shapes]
         + [jax.ShapeDtypeStruct((steps, 6, 8, channels), f32)],
-        in_specs=[vmem] * 10,
+        in_specs=[pl.BlockSpec(memory_space=pl.ANY), pl.BlockSpec(memory_space=pltpu.SMEM)]
+        + [vmem] * 8,
         out_specs=[vmem] * 8,
         scratch_shapes=[
             pltpu.VMEM((small, channels), bf16),
@@ -412,6 +453,8 @@
             pltpu.VMEM(square, f32),
             pltpu.VMEM((1, channels), f32),
             pltpu.VMEM((steps, 8, channels), f32),
+            pltpu.VMEM((2 * steps, places, channels), bf16),
+            pltpu.SemaphoreType.DMA((steps,)),
             pltpu.SemaphoreType.DMA((steps, 4, tiles + 1)),
             pltpu.SemaphoreType.DMA((steps, 4, tiles + 1)),
             pltpu.SemaphoreType.DMA((steps, 4, tiles)),
@@ -423,11 +466,12 @@
             collective_id=0, has_side_effects=True, vmem_limit_bytes=50 * 1024 * 1024
         ),
     )(
-        reals, seed, latent_bank,
+        reals, latent_seed[0, 0], latent_bank,
         g_in[0, 0], g_base[0, 0], g_one[0, 0], g_two[0, 0], d_one[0, 0], d_two[0, 0],
         d_out.reshape(1, channels),
     )
     verdicts = outs[7][:, :, :2, 0].reshape(1, 1, steps, 12)
+    outs = hand_over(outs[:7])
     finals = [member[None, None] for member in outs[:6]] + [outs[6].reshape(1, 1, channels)]
     return (*finals, verdicts)
 

time: 106 us -> 155 us (1.46)
  Pallas kernels: 96.9 us -> 147 us
  local copies, waits for them, and re-layouts: 8.55 us -> 6.43 us
    pallas_call x1, Pallas kernels: 4.03 us -> 33.7 us  [pick(): pl.pallas_call(pick_kernel, out_shape=jax.ShapeDtypeStruct((count,) + dat...]
    pallas_call x0 -> x1, Pallas kernels: none -> 27 us  [hand_over(): pl.pallas_call(functools.partial(hand_over_kernel, count), out_shape=[jax...]
    pallas_call x1, Pallas kernels: 92.9 us -> 86.4 us  [on_device(): pl.pallas_call(functools.partial(train_kernel, rows_count, cols_count, st...]
    unnamed x25 -> x34, local copies, waits for them, and re-layouts: 5.7 us -> 5.7 us
where the time goes in v2:
time: 155 us; the launch traced here: 154 us
  Pallas kernels  147 us (95%)
  local copies, waits for them, and re-layouts  6.43 us (4%)
    pallas_call x1, Pallas kernels, on_device(): pl.pallas_call(functools.partial(train_kernel, rows_count, cols_count, st...  86.4 us
    pallas_call x1, Pallas kernels, pick(): pl.pallas_call(pick_kernel, out_shape=jax.ShapeDtypeStruct((count,) + dat...  33.7 us
    pallas_call x1, Pallas kernels, hand_over(): pl.pallas_call(functools.partial(hand_over_kernel, count), out_shape=[jax...  27 us
    unnamed x34, local copies, waits for them, and re-layouts  5.7 us

profile of v2, /device:TPU:0, one launch (start us, length us, event | category | flops | bytes accessed | tf_op | source)
XLA Modules:
  0.0 154.4 jit_solution(95538307476914453)
XLA Ops:
  0.6 0.0 copy-start.16
  0.6 0.0 copy-start.8
  0.7 0.0 copy-start.7
  0.7 0.0 copy-start.6
  0.7 0.0 copy-start.5
  0.7 0.0 copy-start.2
  0.7 0.0 copy-start.4
  0.7 0.0 copy-start.3
  0.7 0.0 copy-start.14
  0.7 33.7 %shard_map.170.reals_hbm = bf16[4,1024,128]{2,1,0:T(8,128)(2,1)} custom-call(s32[2,2]{1,0:T(2,128)} %bitcast.26, bf16[32,1024,128]{2,1,0:T(8,128)(2,1)} %bitcast.25), custom_call_target="tpu_custom_call" | custom-call | tf_op jit(solution)/shard_map/pallas_call | solution.py:376
  34.5 0.0 copy-done.16
  34.5 0.0 copy-done.8
  34.5 0.0 copy-done.7
  34.5 0.0 copy-done.6
  34.5 0.0 copy-done.5
  34.5 0.0 copy-done.2
  34.5 0.0 copy-done.4
  34.5 0.0 copy-done.3
  34.5 0.0 copy-done.14
  34.5 0.0 copy-start
  34.6 1.2 copy-done
  35.8 86.4 %shard_map.171 = (f32[128,128]{1,0:T(8,128)S(1)}, f32[1024,128]{1,0:T(8,128)S(1)}, f32[128,128]{1,0:T(8,128)S(1)}, f32[128,128]{1,0:T(8,128)S(1)}, f32[128,128]{...) custom-call(bf16[4,1024,128]{2,1,0:T(8,128)(2,1)S(1)} %copy-done, ...), custom_call_target="tpu_custom_call" | custom-call | tf_op jit(solution)/shard_map/pallas_call | solution.py:424
  122.2 0.8 copy-done.1
  123.0 0.6 copy-done.9
  123.6 0.6 copy-done.10
  124.3 0.6 copy-done.11
  124.9 0.6 copy-done.12
  125.5 0.6 copy-done.13
  126.2 0.5 copy-done.15
  126.7 27.0 %shard_map.172 = (f32[128,128]{1,0:T(8,128)}, f32[1024,128]{1,0:T(8,128)}, f32[128,128]{1,0:T(8,128)}, f32[128,128]{1,0:T(8,128)}, f32[128,128]{1,0:T(8,128)}, /*index=5*/f32[128,128]{1,0:T(8,128)}, f32[1,128]{1,0:T(1,128)}) custom-call(f32[128,128]{1,0:T(8,128)} %copy-done.9, f32[1024,128]{1,0:T(8,128)} %copy-done.1, f32[128,128]{1,0:T(8,128)} %copy-done.10, ...), custom_call_target="tpu_custom_call" | custom-call | tf_op jit(solution)/shard_map/pallas_call | solution.py:401
  153.7 0.1 slice_reduce_fusion
  153.7 0.7 reshape_squeeze.3
  (7 shorter events, 0.0 us)
Async XLA Ops:
  0.6 33.8 %copy-start.16 = (f32[1,1,128]{2,1,0:T(1,128)S(1)}, f32[1,1,128]{2,1,0:T(1,128)}, u32[]{:S(2)}) copy-start(f32[1,1,128]{2,1,0:T(1,128)} %param.21) | copy-start | bytes 1540
  0.6 33.8 %copy-start.8 = (f32[1,1,128,128]{3,2,1,0:T(8,128)S(1)}, f32[1,1,128,128]{3,2,1,0:T(8,128)}, u32[]{:S(2)}) copy-start(f32[1,1,128,128]{3,2,1,0:T(8,128)} %param.20) | copy-start | bytes 196612
  0.7 33.8 %copy-start.7 = (f32[1,1,128,128]{3,2,1,0:T(8,128)S(1)}, f32[1,1,128,128]{3,2,1,0:T(8,128)}, u32[]{:S(2)}) copy-start(f32[1,1,128,128]{3,2,1,0:T(8,128)} %param.19) | copy-start | bytes 196612
  0.7 33.8 %copy-start.6 = (f32[1,1,128,128]{3,2,1,0:T(8,128)S(1)}, f32[1,1,128,128]{3,2,1,0:T(8,128)}, u32[]{:S(2)}) copy-start(f32[1,1,128,128]{3,2,1,0:T(8,128)} %param.18) | copy-start | bytes 196612
  0.7 33.8 %copy-start.5 = (f32[1,1,128,128]{3,2,1,0:T(8,128)S(1)}, f32[1,1,128,128]{3,2,1,0:T(8,128)}, u32[]{:S(2)}) copy-start(f32[1,1,128,128]{3,2,1,0:T(8,128)} %param.17) | copy-start | bytes 196612
  0.7 33.8 %copy-start.2 = (f32[1,1,1024,128]{3,2,1,0:T(8,128)S(1)}, f32[1,1,1024,128]{3,2,1,0:T(8,128)}, u32[]{:S(2)}) copy-start(f32[1,1,1024,128]{3,2,1,0:T(8,128)} %param.16) | copy-start | bytes 1572868
  0.7 33.8 %copy-start.4 = (f32[1,1,128,128]{3,2,1,0:T(8,128)S(1)}, f32[1,1,128,128]{3,2,1,0:T(8,128)}, u32[]{:S(2)}) copy-start(f32[1,1,128,128]{3,2,1,0:T(8,128)} %param.15) | copy-start | bytes 196612
  0.7 33.8 %copy-start.3 = (f32[256,128]{1,0:T(8,128)S(1)}, f32[256,128]{1,0:T(8,128)}, u32[]{:S(2)}) copy-start(f32[256,128]{1,0:T(8,128)} %bank_ref.1) | copy-start | bytes 393220
  0.7 33.8 %copy-start.14 = (s32[1,1,2,2]{3,2,1,0:T(2,128)S(1)}, s32[1,1,2,2]{3,2,1,0:T(2,128)}, u32[]{:S(2)}) copy-start(s32[1,1,2,2]{3,2,1,0:T(2,128)} %param.13) | copy-start | bytes 52
  34.5 1.2 copy-start
  122.2 0.8 copy-start.1
  123.0 0.6 copy-start.9
  123.6 0.6 copy-start.10
  124.3 0.6 copy-start.11
  124.9 0.6 copy-start.12
  125.5 0.6 copy-start.13
  126.1 0.5 copy-start.15

commit v3 on v2

--- a/solution.py
+++ b/solution.py
@@ -54,15 +54,11 @@
     )
 
 
-def opposite(way):
-    return way + 1 - 2 * lax.rem(way, 2)
-
-
 def train_kernel(
     rows_count,
     cols_count,
     steps,
-    reals_hbm, seed_ref, bank_ref,
+    reals_ref, seed_ref, bank_ref,
     g_in_ref, g_base_ref, g_one_ref, g_two_ref, d_one_ref, d_two_ref, d_out_ref,
     n_in, n_base, n_one, n_two, n_done, n_dtwo, n_dout, verdict_ref,
     small_own, base_own, small_in, base_in,
@@ -71,7 +67,7 @@
     one_b, two_b, one_tb, two_tb, own_one_tb, own_two_tb,
     d1_b, d2_b, d1_tb, d2_tb,
     acc_one, acc_two, acc_feat, sum_done, sum_dtwo, sum_dout,
-    latent_s, reals_ref, real_sem,
+    latent_s,
     fwd_send, fwd_recv, ret_send, ret_recv, sc_send, sc_recv,
 ):
     places, channels = g_base_ref.shape
@@ -79,55 +75,81 @@
     my_row = lax.axis_index("row")
     my_col = lax.axis_index("col")
 
-    def device_of(way):
-        along = 2 * lax.rem(way, 2) - 1
-        vertical = 1 - way // 2
-        row = lax.rem(my_row + along * vertical + rows_count, rows_count)
-        col = lax.rem(my_col + along * (1 - vertical) + cols_count, cols_count)
-        return (row, col)
+    relayed = rows_count == 4
+    first_slot = 1 if relayed else 0
+
+    def peer(slot):
+        col = lax.rem(my_col + jnp.where(slot == 2, cols_count - 1, 1), cols_count)
+        if relayed:
+            zero = lax.rem(my_row + 2, 4)
+            one = my_row + 1 - 2 * lax.rem(my_row, 2)
+        else:
+            zero = lax.rem(my_row + rows_count - 1, rows_count)
+            one = lax.rem(my_row + 1, rows_count)
+        row = jnp.where(slot == 0, zero, jnp.where(slot == 1, one, my_row))
+        return (row, jnp.where(slot < 2, my_col, col))
+
+    def far(slot):
+        turned = slot + 1 - 2 * lax.rem(slot, 2)
+        return jnp.where(slot < 2, slot, turned) if relayed else turned
+
+    def place_of(slot):
+        if not relayed:
+            return slot + 1
+        odd = lax.rem(my_row, 2)
+        return jnp.where(slot == 0, 1 + odd, jnp.where(slot == 1, 2 - odd, slot + 1))
 
     def rows_of(tile):
         return pl.ds(pl.multiple_of(tile * TILE, TILE), TILE)
 
-    def small_copy(step, way, slot):
+    def small_copy(step, slot, source):
         return pltpu.make_async_remote_copy(
+            src_ref=source, dst_ref=small_in.at[step, far(slot)],
+            send_sem=fwd_send.at[step, slot, 0], recv_sem=fwd_recv.at[step, far(slot), 0],
+            device_id=peer(slot), device_id_type=MESH,
+        )
+
+    def base_copy(step, slot, tile, source):
+        return pltpu.make_async_remote_copy(
+            src_ref=source, dst_ref=base_in.at[step, far(slot), rows_of(tile)],
+            send_sem=fwd_send.at[step, slot, tile + 1],
+            recv_sem=fwd_recv.at[step, far(slot), tile + 1],
+            device_id=peer(slot), device_id_type=MESH,
+        )
+
+    def small_came(step, slot):
+        pltpu.make_async_remote_copy(
             src_ref=small_own, dst_ref=small_in.at[step, slot],
-            send_sem=fwd_send.at[step, way, 0], recv_sem=fwd_recv.at[step, slot, 0],
-            device_id=device_of(way), device_id_type=MESH,
-        )
-
-    def base_copy(step, way, slot, tile):
+            send_sem=fwd_send.at[step, slot, 0], recv_sem=fwd_recv.at[step, slot, 0],
+            device_id=peer(slot), device_id_type=MESH,
+        ).wait_recv()
+
+    def base_came(step, slot, tile):
+        pltpu.make_async_remote_copy(
+            src_ref=base_own.at[rows_of(tile)], dst_ref=base_in.at[step, slot, rows_of(tile)],
+            send_sem=fwd_send.at[step, slot, tile + 1], recv_sem=fwd_recv.at[step, slot, tile + 1],
+            device_id=peer(slot), device_id_type=MESH,
+        ).wait_recv()
+
+    def cot_copy(step, slot, there, tile):
         return pltpu.make_async_remote_copy(
-            src_ref=base_own.at[rows_of(tile)], dst_ref=base_in.at[step, slot, rows_of(tile)],
-            send_sem=fwd_send.at[step, way, tile + 1], recv_sem=fwd_recv.at[step, slot, tile + 1],
-            device_id=device_of(way), device_id_type=MESH,
-        )
-
-    def cot_copy(step, way, slot, tile):
+            src_ref=cot_out.at[step, slot, rows_of(tile)],
+            dst_ref=cot_in.at[step, there, rows_of(tile)],
+            send_sem=ret_send.at[step, slot, tile], recv_sem=ret_recv.at[step, there, tile],
+            device_id=peer(slot), device_id_type=MESH,
+        )
+
+    def scale_copy(step, slot, there):
         return pltpu.make_async_remote_copy(
-            src_ref=cot_out.at[step, way, rows_of(tile)],
-            dst_ref=cot_in.at[step, slot, rows_of(tile)],
-            send_sem=ret_send.at[step, way, tile], recv_sem=ret_recv.at[step, slot, tile],
-            device_id=device_of(way), device_id_type=MESH,
-        )
-
-    def scale_copy(step, way, slot):
-        return pltpu.make_async_remote_copy(
-            src_ref=scale_out.at[step, way], dst_ref=scale_in.at[step, slot],
-            send_sem=sc_send.at[step, way], recv_sem=sc_recv.at[step, slot],
-            device_id=device_of(way), device_id_type=MESH,
-        )
-
-    def real_copy(step):
-        pair = pl.ds(2 * step, 2)
-        return pltpu.make_async_copy(reals_hbm.at[pair], reals_ref.at[pair], real_sem.at[step])
+            src_ref=scale_out.at[step, slot], dst_ref=scale_in.at[step, there],
+            send_sem=sc_send.at[step, slot], recv_sem=sc_recv.at[step, there],
+            device_id=peer(slot), device_id_type=MESH,
+        )
 
     barrier = pltpu.get_barrier_semaphore()
-    for way in range(4):
-        pl.semaphore_signal(barrier, inc=1, device_id=device_of(way), device_id_type=MESH)
-
-    for step in range(steps):
-        real_copy(step).start()
+    for slot in range(4):
+        pl.semaphore_signal(barrier, inc=1, device_id=peer(slot), device_id_type=MESH)
+
     n_in[...] = g_in_ref[...]
     n_base[...] = g_base_ref[...]
     n_one[...] = g_one_ref[...]
@@ -219,17 +241,31 @@
             axis=0,
         ).astype(bf16)
 
-        def send_ways(way, carry):
-            small_copy(step, way, opposite(way)).start()
+        def send_smalls(slot, carry):
+            small_copy(step, slot, small_own).start()
             return carry
 
-        def send_bases(at, carry):
-            way = lax.rem(at, 4)
-            base_copy(step, way, opposite(way), at // 4).start()
-            return carry
-
-        lax.fori_loop(0, 4, send_ways, 0)
-        lax.fori_loop(0, 4 * tiles, send_bases, 0)
+        def send_bases(tile, carry):
+            def send(slot, carry):
+                base_copy(step, slot, tile, base_own.at[rows_of(tile)]).start()
+                return carry
+
+            return lax.fori_loop(first_slot, 4, send, carry)
+
+        def pass_on(tile):
+            if relayed:
+                @pl.when(tile == 0)
+                def _():
+                    small_came(step, 1)
+                    small_copy(step, 0, small_in.at[step, 1]).start()
+
+                @pl.when(tile < tiles)
+                def _():
+                    base_came(step, 1, tile)
+                    base_copy(step, 0, tile, base_in.at[step, 1, rows_of(tile)]).start()
+
+        lax.fori_loop(first_slot, 4, send_smalls, 0)
+        lax.fori_loop(0, tiles, send_bases, 0)
 
         put_blocks(one_b, n_one[...].astype(bf16))
         put_blocks(two_b, n_two[...].astype(bf16))
@@ -256,21 +292,40 @@
         lax.fori_loop(0, tiles, own_tile, 0)
         scale_own[...] = settle(step, 0, False)
 
+        pass_on(jnp.int32(0))
+
         clear()
-        real_copy(step).wait()
 
         def real_tile(tile, carry):
             at = rows_of(tile)
             judge_tile(pair_lanes(reals_ref[2 * step, at], reals_ref[2 * step + 1, at]), d_out_pair)
+            pass_on(tile + 1)
             return carry
 
         lax.fori_loop(0, tiles, real_tile, 0)
         settle(step, 5, True)
 
-        def beside(order, carry):
-            way = 3 - order
-            small_copy(step, way, way).wait_recv()
-            small = small_in.at[step, way]
+        def add_partner(tile):
+            @pl.when(tile == 0)
+            def _():
+                scale_copy(step, 0, 0).wait_recv()
+
+            at = rows_of(tile)
+            cot_copy(step, 0, 0, tile).wait_recv()
+            total = cot_out[step, 1, at].astype(f32) * scale_out[step, 1, 0:1]
+            total += cot_in[step, 0, at].astype(f32) * scale_in[step, 0, 0:1]
+            cot_out[step, 1, at] = total.astype(bf16)
+            cot_copy(step, 1, 1, tile).start()
+
+        def beside(slot, carry):
+            def came():
+                small_came(step, slot)
+
+            if relayed:
+                pl.when(slot != 1)(came)
+            else:
+                came()
+            small = small_in.at[step, slot]
             put_blocks(one_b, small[0:channels])
             put_blocks(two_b, small[channels : 2 * channels])
             shift_a, shift_b = shifts_of(small)
@@ -278,16 +333,37 @@
 
             def their_tile(tile, carry):
                 at = rows_of(tile)
-                base_copy(step, way, way, tile).wait_recv()
-                images = made(base_in[step, way, at], shift_a, shift_b, one_b[...], two_b[...], None)
+
+                def came():
+                    base_came(step, slot, tile)
+
+                def back():
+                    cot_copy(step, slot, far(slot), tile).start()
+
+                if relayed:
+                    pl.when(slot != 1)(came)
+                else:
+                    came()
+                images = made(base_in[step, slot, at], shift_a, shift_b, one_b[...], two_b[...], None)
                 outer, inner = judge_tile(images, d_out_pair)
-                cot_out[step, way, at] = (outer + dot(inner, d1_tb[...])).astype(bf16)
-                cot_copy(step, way, opposite(way), tile).start()
+                cot_out[step, slot, at] = (outer + dot(inner, d1_tb[...])).astype(bf16)
+                if relayed:
+                    pl.when(slot != 1)(back)
+                    pl.when(slot == 2)(lambda: add_partner(tile))
+                else:
+                    back()
                 return carry
 
             lax.fori_loop(0, tiles, their_tile, 0)
-            scale_out[step, way] = settle(step, way + 1, False)
-            scale_copy(step, way, opposite(way)).start()
+            scale_out[step, slot] = settle(step, place_of(slot), False)
+
+            def back_scale():
+                scale_copy(step, slot, far(slot)).start()
+
+            if relayed:
+                pl.when(slot != 1)(back_scale)
+            else:
+                back_scale()
             return carry
 
         lax.fori_loop(0, 4, beside, 0)
@@ -298,23 +374,25 @@
 
         clear()
 
-        def scale_waits(way, carry):
-            scale_copy(step, way, way).wait_recv()
+        def scale_waits(slot, carry):
+            scale_copy(step, slot, slot).wait_recv()
             return carry
 
-        lax.fori_loop(0, 4, scale_waits, 0)
+        lax.fori_loop(2 if relayed else 0, 4, scale_waits, 0)
 
         def back_tile(tile, carry):
             at = rows_of(tile)
 
-            def cot_waits(way, carry):
-                cot_copy(step, way, way, tile).wait_recv()
+            def cot_waits(slot, carry):
+                cot_copy(step, slot, slot, tile).wait_recv()
                 return carry
 
-            lax.fori_loop(0, 4, cot_waits, 0)
+            lax.fori_loop(first_slot, 4, cot_waits, 0)
             total = cot_own[at].astype(f32) * scale_own[0:1]
-            for way in range(4):
-                total += cot_in[step, way, at].astype(f32) * scale_in[step, way, 0:1]
+            if relayed:
+                total += cot_in[step, 1, at].astype(f32)
+            for slot in range(2 if relayed else 0, 4):
+                total += cot_in[step, slot, at].astype(f32) * scale_in[step, slot, 0:1]
             half = total.astype(bf16)
             acc_two[...] += rows_dot(middle_s[at], half)
             inner = (dot(half, own_two_tb[...]) * slope_mid_s[at]).astype(bf16)
@@ -340,13 +418,20 @@
             precision=lax.Precision.HIGHEST, preferred_element_type=f32,
         )
 
-        def sent(way, carry):
-            small_copy(step, way, way).wait_send()
-            scale_copy(step, way, way).wait_send()
+        def sent(slot, carry):
+            small_copy(step, slot, small_own).wait_send()
+
+            def scale_sent():
+                scale_copy(step, slot, far(slot)).wait_send()
+
+            if relayed:
+                pl.when(slot != 1)(scale_sent)
+            else:
+                scale_sent()
 
             def sent_tile(tile, carry):
-                base_copy(step, way, way, tile).wait_send()
-                cot_copy(step, way, way, tile).wait_send()
+                base_copy(step, slot, tile, base_own.at[rows_of(tile)]).wait_send()
+                cot_copy(step, slot, far(slot), tile).wait_send()
                 return carry
 
             return lax.fori_loop(0, tiles, sent_tile, carry)
@@ -379,31 +464,25 @@
         in_specs=[
             pl.BlockSpec(memory_space=pltpu.SMEM), pl.BlockSpec(memory_space=pl.ANY)
         ],
-        out_specs=pl.BlockSpec(memory_space=pl.ANY),
+        out_specs=pl.BlockSpec(memory_space=pltpu.VMEM),
         scratch_shapes=[pltpu.SemaphoreType.DMA((count,))],
         compiler_params=pltpu.CompilerParams(vmem_limit_bytes=58 * 1024 * 1024),
     )(index, data)
 
 
 def hand_over_kernel(count, *refs):
-    copies = [
-        pltpu.make_async_copy(refs[i], refs[count + i], refs[-1].at[i]) for i in range(count)
-    ]
-    for copy in copies:
-        copy.start()
-    for copy in copies:
-        copy.wait()
+    for i in range(count):
+        refs[count + i][...] = refs[i][...]
 
 
 def hand_over(members):
     count = len(members)
-    anywhere = pl.BlockSpec(memory_space=pl.ANY)
+    vmem = pl.BlockSpec(memory_space=pltpu.VMEM)
     return pl.pallas_call(
         functools.partial(hand_over_kernel, count),
         out_shape=[jax.ShapeDtypeStruct(member.shape, member.dtype) for member in members],
-        in_specs=[anywhere] * count,
-        out_specs=[anywhere] * count,
-        scratch_shapes=[pltpu.SemaphoreType.DMA((count,))],
+        in_specs=[vmem] * count,
+        out_specs=[vmem] * count,
     )(*members)
 
 
@@ -425,8 +504,7 @@
         functools.partial(train_kernel, rows_count, cols_count, steps),
         out_shape=[jax.ShapeDtypeStruct(shape, f32) for shape in shapes]
         + [jax.ShapeDtypeStruct((steps, 6, 8, channels), f32)],
-        in_specs=[pl.BlockSpec(memory_space=pl.ANY), pl.BlockSpec(memory_space=pltpu.SMEM)]
-        + [vmem] * 8,
+        in_specs=[vmem, pl.BlockSpec(memory_space=pltpu.SMEM)] + [vmem] * 8,
         out_specs=[vmem] * 8,
         scratch_shapes=[
             pltpu.VMEM((small, channels), bf16),
@@ -453,8 +531,6 @@
             pltpu.VMEM(square, f32),
             pltpu.VMEM((1, channels), f32),
             pltpu.VMEM((steps, 8, channels), f32),
-            pltpu.VMEM((2 * steps, places, channels), bf16),
-            pltpu.SemaphoreType.DMA((steps,)),
             pltpu.SemaphoreType.DMA((steps, 4, tiles + 1)),
             pltpu.SemaphoreType.DMA((steps, 4, tiles + 1)),
             pltpu.SemaphoreType.DMA((steps, 4, tiles)),

time: 155 us -> 92.8 us (0.60)
  Pallas kernels: 147 us -> 85.4 us
    pallas_call x1, Pallas kernels: 33.7 us -> 3.02 us  [pick(): pl.pallas_call(pick_kernel, out_shape=jax.ShapeDtypeStruct((count,) + dat...]
    pallas_call x1, Pallas kernels: 27 us -> 2 us  [hand_over(): pl.pallas_call(functools.partial(hand_over_kernel, count), out_shape=[jax...]
    pallas_call x1, Pallas kernels: 86.4 us -> 80.3 us  [on_device(): pl.pallas_call(functools.partial(train_kernel, rows_count, cols_count, st...]
where the time goes in v3:
time: 92.8 us; the launch traced here: 92.6 us
  Pallas kernels  85.4 us (92%)
  local copies, waits for them, and re-layouts  6.43 us (7%)
    pallas_call x1, Pallas kernels, on_device(): pl.pallas_call(functools.partial(train_kernel, rows_count, cols_count, st...  80.3 us
    unnamed x34, local copies, waits for them, and re-layouts  5.7 us
    pallas_call x1, Pallas kernels, pick(): pl.pallas_call(pick_kernel, out_shape=jax.ShapeDtypeStruct((count,) + dat...  3.02 us
    pallas_call x1, Pallas kernels, hand_over(): pl.pallas_call(functools.partial(hand_over_kernel, count), out_shape=[jax...  2 us

profile of v3, /device:TPU:0, one launch (start us, length us, event | category | flops | bytes accessed | tf_op | source)
XLA Modules:
  0.0 92.6 jit_solution(16530994588544548976)
XLA Ops:
  0.6 0.0 copy-start.16
  0.6 0.0 copy-start.8
  0.7 0.0 copy-start.7
  0.7 0.0 copy-start.6
  0.7 0.0 copy-start.5
  0.7 0.0 copy-start.2
  0.7 0.0 copy-start.4
  0.7 0.0 copy-start.3
  0.7 0.0 copy-start.14
  0.7 3.0 %shard_map.170.reals_ref = bf16[4,1024,128]{2,1,0:T(8,128)(2,1)} custom-call(s32[2,2]{1,0:T(2,128)} %bitcast.26, bf16[32,1024,128]{2,1,0:T(8,128)(2,1)} %bitcast.25), custom_call_target="tpu_custom_call" | custom-call | tf_op jit(solution)/shard_map/pallas_call | solution.py:461
  3.8 0.0 copy-done.16
  3.8 0.0 copy-done.8
  3.8 0.0 copy-done.7
  3.8 0.0 copy-done.6
  3.8 0.0 copy-done.5
  3.8 0.0 copy-done.2
  3.8 0.0 copy-done.4
  3.8 0.0 copy-done.3
  3.8 0.0 copy-done.14
  3.9 1.2 %copy-done = bf16[4,1024,128]{2,1,0:T(8,128)(2,1)S(1)} copy-done((bf16[4,1024,128]{2,1,0:T(8,128)(2,1)S(1)}, bf16[4,1024,128]{2,1,0:T(8,128)(2,1)}, u32[]{:S(2)}) %copy-start) | copy-done | bytes 1048600
  5.1 80.3 %shard_map.171 = (f32[128,128]{1,0:T(8,128)S(1)}, f32[1024,128]{1,0:T(8,128)S(1)}, f32[128,128]{1,0:T(8,128)S(1)}, f32[128,128]{1,0:T(8,128)S(1)}, f32[128,128]{...) custom-call(bf16[4,1024,128]{2,1,0:T(8,128)(2,1)S(1)} %copy-done, ...), custom_call_target="tpu_custom_call" | custom-call | tf_op jit(solution)/shard_map/pallas_call | solution.py:503
  85.4 0.0 copy-start.1
  85.4 0.8 copy-done.1
  86.2 0.6 copy-done.9
  86.8 0.6 copy-done.10
  87.5 0.6 copy-done.11
  88.1 0.6 copy-done.12
  88.7 0.6 copy-done.13
  89.4 0.5 copy-done.15
  89.9 2.0 %shard_map.172 = (f32[128,128]{1,0:T(8,128)}, f32[1024,128]{1,0:T(8,128)}, f32[128,128]{1,0:T(8,128)}, f32[128,128]{1,0:T(8,128)}, f32[128,128]{1,0:T(8,128)}, /*index=5*/f32[128,128]{1,0:T(8,128)}, f32[1,128]{1,0:T(1,128)}) custom-call(f32[128,128]{1,0:T(8,128)} %copy-done.9, f32[1024,128]{1,0:T(8,128)} %copy-done.1, f32[128,128]{1,0:T(8,128)} %copy-done.10, ...), custom_call_target="tpu_custom_call" | custom-call | tf_op jit(solution)/shard_map/pallas_call | solution.py:481
  91.9 0.1 slice_reduce_fusion
  92.0 0.7 reshape_squeeze.3
  (7 shorter events, 0.0 us)
Async XLA Ops:
  0.6 3.1 %copy-start.16 = (f32[1,1,128]{2,1,0:T(1,128)S(1)}, f32[1,1,128]{2,1,0:T(1,128)}, u32[]{:S(2)}) copy-start(f32[1,1,128]{2,1,0:T(1,128)} %param.21) | copy-start | bytes 1540
  0.6 3.1 %copy-start.8 = (f32[1,1,128,128]{3,2,1,0:T(8,128)S(1)}, f32[1,1,128,128]{3,2,1,0:T(8,128)}, u32[]{:S(2)}) copy-start(f32[1,1,128,128]{3,2,1,0:T(8,128)} %param.20) | copy-start | bytes 196612
  0.7 3.1 %copy-start.7 = (f32[1,1,128,128]{3,2,1,0:T(8,128)S(1)}, f32[1,1,128,128]{3,2,1,0:T(8,128)}, u32[]{:S(2)}) copy-start(f32[1,1,128,128]{3,2,1,0:T(8,128)} %param.19) | copy-start | bytes 196612
  0.7 3.1 %copy-start.6 = (f32[1,1,128,128]{3,2,1,0:T(8,128)S(1)}, f32[1,1,128,128]{3,2,1,0:T(8,128)}, u32[]{:S(2)}) copy-start(f32[1,1,128,128]{3,2,1,0:T(8,128)} %param.18) | copy-start | bytes 196612
  0.7 3.1 %copy-start.5 = (f32[1,1,128,128]{3,2,1,0:T(8,128)S(1)}, f32[1,1,128,128]{3,2,1,0:T(8,128)}, u32[]{:S(2)}) copy-start(f32[1,1,128,128]{3,2,1,0:T(8,128)} %param.17) | copy-start | bytes 196612
  0.7 3.1 %copy-start.2 = (f32[1,1,1024,128]{3,2,1,0:T(8,128)S(1)}, f32[1,1,1024,128]{3,2,1,0:T(8,128)}, u32[]{:S(2)}) copy-start(f32[1,1,1024,128]{3,2,1,0:T(8,128)} %param.16) | copy-start | bytes 1572868
  0.7 3.1 %copy-start.4 = (f32[1,1,128,128]{3,2,1,0:T(8,128)S(1)}, f32[1,1,128,128]{3,2,1,0:T(8,128)}, u32[]{:S(2)}) copy-start(f32[1,1,128,128]{3,2,1,0:T(8,128)} %param.15) | copy-start | bytes 196612
  0.7 3.1 %copy-start.3 = (f32[256,128]{1,0:T(8,128)S(1)}, f32[256,128]{1,0:T(8,128)}, u32[]{:S(2)}) copy-start(f32[256,128]{1,0:T(8,128)} %bank_ref.1) | copy-start | bytes 393220
  0.7 3.1 %copy-start.14 = (s32[1,1,2,2]{3,2,1,0:T(2,128)S(1)}, s32[1,1,2,2]{3,2,1,0:T(2,128)}, u32[]{:S(2)}) copy-start(s32[1,1,2,2]{3,2,1,0:T(2,128)} %param.13) | copy-start | bytes 52
  3.8 1.2 %copy-start = (bf16[4,1024,128]{2,1,0:T(8,128)(2,1)S(1)}, bf16[4,1024,128]{2,1,0:T(8,128)(2,1)}, u32[]{:S(2)}) copy-start(bf16[4,1024,128]{2,1,0:T(8,128)(2,1)} %shard_map.170.reals_ref) | copy-start | bytes 3145732
  85.4 0.8 copy-start.1
  86.2 0.6 copy-start.9
  86.8 0.6 copy-start.10
  87.5 0.6 copy-start.11
  88.1 0.6 copy-start.12
  88.7 0.6 copy-start.13
  89.4 0.5 copy-start.15

commit v4 on v3

--- a/solution.py
+++ b/solution.py
@@ -11,6 +11,7 @@
 base_rate = 0.1
 
 TILE = 512
+SLAB = 32
 MESH = pl.DeviceIdType.MESH
 f32 = jnp.float32
 bf16 = jnp.bfloat16
@@ -33,6 +34,14 @@
     twice = 1.0 + jnp.tanh(half)
     act = half * twice
     return act, twice * ((1.0 + values) - act)
+
+
+def by_slabs(function, *arrays):
+    parts = [
+        function(*(member[at : at + SLAB] for member in arrays))
+        for at in range(0, arrays[0].shape[0], SLAB)
+    ]
+    return tuple(jnp.concatenate(list(piece), axis=0) for piece in zip(*parts))
 
 
 def pair_lanes(left, right):
@@ -173,33 +182,55 @@
         return hi[0:1] + hi[2:3] + hi[4:5], hi[1:2] + hi[3:4] + hi[5:6]
 
     def made(base, shift_a, shift_b, one, two, keep):
-        base = base.astype(f32)
-        gen_pre = pair_lanes(base + shift_a, base + shift_b)
-        act, slope = silu_parts(gen_pre)
-        hidden = act.astype(bf16)
-        middle_pre = dot(hidden, one)
-        act_mid, slope_mid = silu_parts(middle_pre)
-        middle = act_mid.astype(bf16)
+        def enter(rows):
+            rows = rows.astype(f32)
+            act, slope = silu_parts(pair_lanes(rows + shift_a, rows + shift_b))
+            return act.astype(bf16), slope
+
+        def halfway(rows):
+            act, slope = silu_parts(rows)
+            return act.astype(bf16), slope
+
+        def leave(hidden_rows, rows):
+            return ((hidden_rows.astype(f32) + rows).astype(bf16),)
+
+        hidden, slope = by_slabs(enter, base)
+        middle, slope_mid = by_slabs(halfway, dot(hidden, one))
         if keep is not None:
             hidden_s[keep] = hidden
             middle_s[keep] = middle
             slope_pre_s[keep] = slope
             slope_mid_s[keep] = slope_mid
-        return (hidden.astype(f32) + dot(middle, two)).astype(bf16)
+        return by_slabs(leave, hidden, dot(middle, two))[0]
 
     def judge_tile(images, d_out_pair):
-        first_pre = dot(images, d1_b[...])
-        act, slope_first = silu_parts(first_pre)
-        first = act.astype(bf16)
-        summed = images.astype(f32) + dot(first, d2_b[...])
-        feature, slope_sum = silu_parts(summed)
-        acc_feat[...] += jnp.sum(feature, axis=0, keepdims=True)
-        outer = slope_sum * d_out_pair
-        outer_half = outer.astype(bf16)
-        inner = (dot(outer_half, d2_tb[...]) * slope_first).astype(bf16)
+        def halfway(rows):
+            act, slope = silu_parts(rows)
+            return act.astype(bf16), slope
+
+        def leave(image_rows, rows):
+            feature, slope = silu_parts(image_rows.astype(f32) + rows)
+            outer = slope * d_out_pair
+            return outer, outer.astype(bf16), jnp.sum(
+                feature.reshape(SLAB // 8, 8, 2 * channels), axis=0
+            )
+
+        def turn(rows, slope):
+            return ((rows * slope).astype(bf16),)
+
+        first, slope_first = by_slabs(halfway, dot(images, d1_b[...]))
+        outer, outer_half, feature_sums = by_slabs(leave, images, dot(first, d2_b[...]))
+        acc_feat[...] += jnp.sum(feature_sums, axis=0, keepdims=True)
+        inner = by_slabs(turn, dot(outer_half, d2_tb[...]), slope_first)[0]
         acc_two[...] += rows_dot(first, outer_half)
         acc_one[...] += rows_dot(images, inner)
         return outer, inner
+
+    def returned(outer, inner):
+        def add(outer_rows, rows):
+            return ((outer_rows + rows).astype(bf16),)
+
+        return by_slabs(add, outer, dot(inner, d1_tb[...]))[0]
 
     def clear():
         acc_feat[...] = jnp.zeros_like(acc_feat)
@@ -286,7 +317,7 @@
             at = rows_of(tile)
             images = made(base_own[at], shift[0:1], shift[1:2], one_b[...], two_b[...], at)
             outer, inner = judge_tile(images, d_out_pair)
-            cot_own[at] = (outer + dot(inner, d1_tb[...])).astype(bf16)
+            cot_own[at] = returned(outer, inner)
             return carry
 
         lax.fori_loop(0, tiles, own_tile, 0)
@@ -346,7 +377,7 @@
                     came()
                 images = made(base_in[step, slot, at], shift_a, shift_b, one_b[...], two_b[...], None)
                 outer, inner = judge_tile(images, d_out_pair)
-                cot_out[step, slot, at] = (outer + dot(inner, d1_tb[...])).astype(bf16)
+                cot_out[step, slot, at] = returned(outer, inner)
                 if relayed:
                     pl.when(slot != 1)(back)
                     pl.when(slot == 2)(lambda: add_partner(tile))
@@ -468,22 +499,6 @@
         scratch_shapes=[pltpu.SemaphoreType.DMA((count,))],
         compiler_params=pltpu.CompilerParams(vmem_limit_bytes=58 * 1024 * 1024),
     )(index, data)
-
-
-def hand_over_kernel(count, *refs):
-    for i in range(count):
-        refs[count + i][...] = refs[i][...]
-
-
-def hand_over(members):
-    count = len(members)
-    vmem = pl.BlockSpec(memory_space=pltpu.VMEM)
-    return pl.pallas_call(
-        functools.partial(hand_over_kernel, count),
-        out_shape=[jax.ShapeDtypeStruct(member.shape, member.dtype) for member in members],
-        in_specs=[vmem] * count,
-        out_specs=[vmem] * count,
-    )(*members)
 
 
 def on_device(
@@ -547,7 +562,6 @@
         d_out.reshape(1, channels),
     )
     verdicts = outs[7][:, :, :2, 0].reshape(1, 1, steps, 12)
-    outs = hand_over(outs[:7])
     finals = [member[None, None] for member in outs[:6]] + [outs[6].reshape(1, 1, channels)]
     return (*finals, verdicts)
 

time: 92.8 us -> 90.8 us (0.978)
  Pallas kernels: 85.4 us -> 83.3 us
    pallas_call x1 -> x0, Pallas kernels: 2 us -> none  [hand_over(): pl.pallas_call(functools.partial(hand_over_kernel, count), out_shape=[jax...]
    unnamed x34 -> x27, local copies, waits for them, and re-layouts: 5.7 us -> 5.7 us
where the time goes in v4:
time: 90.8 us; the launch traced here: 90.6 us
  Pallas kernels  83.3 us (92%)
  local copies, waits for them, and re-layouts  6.44 us (7%)
    pallas_call x1, Pallas kernels, on_device(): pl.pallas_call(functools.partial(train_kernel, rows_count, cols_count, st...  80.3 us
    unnamed x27, local copies, waits for them, and re-layouts  5.7 us
    pallas_call x1, Pallas kernels, pick(): pl.pallas_call(pick_kernel, out_shape=jax.ShapeDtypeStruct((count,) + dat...  3.01 us

profile of v4, /device:TPU:0, one launch (start us, length us, event | category | flops | bytes accessed | tf_op | source)
XLA Modules:
  0.0 90.6 jit_solution(12127307997799208489)
XLA Ops:
  0.6 0.0 copy-start.9
  0.6 0.0 copy-start.7
  0.7 0.0 copy-start.6
  0.7 0.0 copy-start.5
  0.7 0.0 copy-start.4
  0.7 0.0 copy-start.1
  0.7 0.0 copy-start.3
  0.7 0.0 copy-start.2
  0.7 0.0 copy-start.8
  0.7 3.0 %shard_map.170.reals_ref = bf16[4,1024,128]{2,1,0:T(8,128)(2,1)} custom-call(s32[2,2]{1,0:T(2,128)} %bitcast.33, bf16[32,1024,128]{2,1,0:T(8,128)(2,1)} %bitcast.32), custom_call_target="tpu_custom_call" | custom-call | tf_op jit(solution)/shard_map/pallas_call | solution.py:492
  3.7 0.0 copy-done.9
  3.8 0.0 copy-done.7
  3.8 0.0 copy-done.6
  3.8 0.0 copy-done.5
  3.8 0.0 copy-done.4
  3.8 0.0 copy-done.1
  3.8 0.0 copy-done.3
  3.8 0.0 copy-done.2
  3.8 0.0 copy-done.8
  3.8 0.0 copy-start
  3.8 1.2 %copy-done = bf16[4,1024,128]{2,1,0:T(8,128)(2,1)S(1)} copy-done((bf16[4,1024,128]{2,1,0:T(8,128)(2,1)S(1)}, bf16[4,1024,128]{2,1,0:T(8,128)(2,1)}, u32[]{:S(2)}) %copy-start) | copy-done | bytes 1048600
  5.1 80.3 %shard_map.171 = (f32[128,128]{1,0:T(8,128)S(1)}, f32[1024,128]{1,0:T(8,128)S(1)}, f32[128,128]{1,0:T(8,128)S(1)}, f32[128,128]{1,0:T(8,128)S(1)}, f32[128,128]{...) custom-call(bf16[4,1024,128]{2,1,0:T(8,128)(2,1)S(1)} %copy-done, ...), custom_call_target="tpu_custom_call" | custom-call | tf_op jit(solution)/shard_map/pallas_call | solution.py:518
  85.4 0.1 slice_reduce_fusion
  85.5 0.7 reshape_squeeze.3
  86.1 0.6 copy.26
  86.7 0.8 copy.27
  87.5 0.6 copy.28
  88.2 0.6 copy.29
  88.8 0.6 copy.30
  89.4 0.6 copy.31
  90.1 0.5 copy.32
Async XLA Ops:
  0.6 3.1 %copy-start.9 = (f32[1,1,128]{2,1,0:T(1,128)S(1)}, f32[1,1,128]{2,1,0:T(1,128)}, u32[]{:S(2)}) copy-start(f32[1,1,128]{2,1,0:T(1,128)} %param.21) | copy-start | bytes 1540
  0.6 3.1 %copy-start.7 = (f32[1,1,128,128]{3,2,1,0:T(8,128)S(1)}, f32[1,1,128,128]{3,2,1,0:T(8,128)}, u32[]{:S(2)}) copy-start(f32[1,1,128,128]{3,2,1,0:T(8,128)} %param.20) | copy-start | bytes 196612
  0.7 3.1 %copy-start.6 = (f32[1,1,128,128]{3,2,1,0:T(8,128)S(1)}, f32[1,1,128,128]{3,2,1,0:T(8,128)}, u32[]{:S(2)}) copy-start(f32[1,1,128,128]{3,2,1,0:T(8,128)} %param.19) | copy-start | bytes 196612
  0.7 3.1 %copy-start.5 = (f32[1,1,128,128]{3,2,1,0:T(8,128)S(1)}, f32[1,1,128,128]{3,2,1,0:T(8,128)}, u32[]{:S(2)}) copy-start(f32[1,1,128,128]{3,2,1,0:T(8,128)} %param.18) | copy-start | bytes 196612
  0.7 3.1 %copy-start.4 = (f32[1,1,128,128]{3,2,1,0:T(8,128)S(1)}, f32[1,1,128,128]{3,2,1,0:T(8,128)}, u32[]{:S(2)}) copy-start(f32[1,1,128,128]{3,2,1,0:T(8,128)} %param.17) | copy-start | bytes 196612
  0.7 3.1 %copy-start.1 = (f32[1,1,1024,128]{3,2,1,0:T(8,128)S(1)}, f32[1,1,1024,128]{3,2,1,0:T(8,128)}, u32[]{:S(2)}) copy-start(f32[1,1,1024,128]{3,2,1,0:T(8,128)} %param.16) | copy-start | bytes 1572868
  0.7 3.1 %copy-start.3 = (f32[1,1,128,128]{3,2,1,0:T(8,128)S(1)}, f32[1,1,128,128]{3,2,1,0:T(8,128)}, u32[]{:S(2)}) copy-start(f32[1,1,128,128]{3,2,1,0:T(8,128)} %param.15) | copy-start | bytes 196612
  0.7 3.1 %copy-start.2 = (f32[256,128]{1,0:T(8,128)S(1)}, f32[256,128]{1,0:T(8,128)}, u32[]{:S(2)}) copy-start(f32[256,128]{1,0:T(8,128)} %bank_ref.1) | copy-start | bytes 393220
  0.7 3.1 %copy-start.8 = (s32[1,1,2,2]{3,2,1,0:T(2,128)S(1)}, s32[1,1,2,2]{3,2,1,0:T(2,128)}, u32[]{:S(2)}) copy-start(s32[1,1,2,2]{3,2,1,0:T(2,128)} %param.13) | copy-start | bytes 52
  3.8 1.2 %copy-start = (bf16[4,1024,128]{2,1,0:T(8,128)(2,1)S(1)}, bf16[4,1024,128]{2,1,0:T(8,128)(2,1)}, u32[]{:S(2)}) copy-start(bf16[4,1024,128]{2,1,0:T(8,128)(2,1)} %shard_map.170.reals_ref) | copy-start | bytes 3145732
